TPU v7x, 32 devices: a whole 2x2x4 slice. The times are simulated.
32 devices in a mesh: bin: 4 (over y, x), grp: 8 (over z, core).
Axes of the slice: x: 2, y: 2, z: 4, core: 2. Of those that a mesh axis runs over, the one named last changes fastest.
Arguments:
- templates: bfloat16 [32768, 512], P(('bin', 'grp')), may hold values from -6 to 6
- owner_device: int32 [32768, 1], P(('bin', 'grp')), may hold values from 0 to 31; in each aligned block of 1024 rows (0 to 1023, 1024 to 2047, ...) at most 64 rows name the same one
- rate_code: int32 [32768], P(('bin', 'grp')), may hold values from 0 to 4
- rate_gains: float32 [5, 512], replicated, may hold values from 0.5 to 2
- sketch: float32 [512, 256], replicated, may hold values from -6 to 6
- strain: float32 [2, 65536], P(None, 'grp'), may hold values from -6 to 6
Outputs:
- mixing: bfloat16 [32768, 256], P(('bin', 'grp'))
- spectrum: float32 [4, 256], P('bin')
- filtered_0: bfloat16 [4, 2, 65536, 256], P('bin', None, 'grp')
- filtered_1: bfloat16 [4, 2, 32768, 256], P('bin', None, 'grp')
- filtered_2: bfloat16 [4, 2, 16384, 256], P('bin', None, 'grp')
- filtered_3: bfloat16 [4, 2, 8192, 256], P('bin', None, 'grp')
- filtered_4: bfloat16 [4, 2, 4096, 256], P('bin', None, 'grp')
Inputs may be any that keep to these rules, and one draw needn't show every extreme that they name: `owner_device`: among the rows of one device, no device is named by more than 64 rows, and some device is named by exactly 64 rows.
All inputs are finite; a program needn't handle non-finite values.
Results may differ from a plain program's by a relative error of at most 0.0059.
Values may be sent and summed in bfloat16 or wider, within the bound.
No kernel may reach another device: no remote copies, remote signals or barrier semaphores. Data moves between devices by JAX's collectives and lax.ppermute only.
A program may use at most 128 MiB of HBM per device.

v0:
```python
import math

import jax
import jax.numpy as jnp
from jax import lax
from jax.sharding import PartitionSpec as P

highest = lax.Precision.HIGHEST
inv_root_two = 0.7071067811865476


def shifted(x, axis, by):
    length = lax.axis_size(axis)
    pairs = [(i, i + by) for i in range(length) if 0 <= i + by < length]
    return lax.ppermute(x, axis, pairs)


def whiten_rows(templates, rate_code, rate_gains):
    factor = jnp.zeros(templates.shape, jnp.float32)
    for rate_level in range(rate_gains.shape[0]):
        factor = factor + jnp.where(
            (rate_code == rate_level)[:, None], rate_gains[rate_level][None, :], jnp.float32(0.0)
        )
    return (templates.astype(jnp.float32) * factor).astype(jnp.bfloat16)


def strain_levels(strain, count):
    current = strain
    level_list = []
    for rate_level in range(count):
        if rate_level > 0:
            paired = current.reshape(current.shape[0], -1, 2)
            current = (paired[:, :, 0] + paired[:, :, 1]) * inv_root_two
        level_list.append(current.astype(jnp.bfloat16))
    return level_list


def filter_level(history, rounded, basis_bf, stride):
    tap_rows = basis_bf[::stride]
    joined = jnp.concatenate([history[:, 1:], rounded], axis=1)
    return lax.conv_general_dilated(
        joined[:, :, None],
        tap_rows[::-1][:, None, :],
        (1,),
        "VALID",
        dimension_numbers=("NWC", "WIO", "NWC"),
        preferred_element_type=jnp.float32,
    )


def basis_from(product):
    inner_gram = jnp.dot(product.T, product, precision=highest)
    lower_factor = jnp.linalg.cholesky(inner_gram)
    basis_bf = jax.scipy.linalg.solve_triangular(lower_factor, product.T, lower=True).T.astype(
        jnp.bfloat16
    )
    return (basis_bf, jnp.diagonal(lower_factor))


def local(templates, owner_device, rate_code, rate_gains, sketch, strain):
    tpl_rows = templates.shape[0]
    slice_len = templates.shape[1]
    group_size = lax.axis_size("grp")
    bin_count = lax.axis_size("bin")
    devices = bin_count * group_size
    capacity = 2 * tpl_rows // devices
    scale_down = tpl_rows * group_size * math.sqrt(slice_len)
    whitened = whiten_rows(templates, rate_code, rate_gains)
    target = owner_device[:, 0]
    member_table = (target[:, None] == jnp.arange(devices, dtype=jnp.int32)[None, :]).astype(
        jnp.int32
    )
    rank_in_dest = jnp.sum(jnp.cumsum(member_table, axis=0) * member_table, axis=1) - 1
    slot_index = target * capacity + rank_in_dest
    outgoing = jnp.zeros((devices * capacity, slice_len), jnp.bfloat16).at[slot_index].set(whitened)
    received = lax.all_to_all(outgoing, ("bin", "grp"), split_axis=0, concat_axis=0, tiled=True)
    partial_gram = lax.dot_general(
        received, received, (((0,), (0,)), ((), ())), preferred_element_type=jnp.float32
    )
    gram_total = lax.psum(partial_gram, "grp")
    product = jnp.dot(gram_total, sketch, precision=highest)
    basis_bf, diag_here = basis_from(product)
    coeffs = jnp.dot(received, basis_bf, preferred_element_type=jnp.float32).astype(jnp.bfloat16)
    returned = lax.all_to_all(coeffs, ("bin", "grp"), split_axis=0, concat_axis=0, tiled=True)
    mixing = returned[slot_index]
    spectrum = (diag_here / scale_down)[None, :]
    levels = strain_levels(strain, rate_gains.shape[0])
    rim_list = [
        levels[rate_level][:, -(slice_len >> rate_level) :] for rate_level in range(len(levels))
    ]
    history = shifted((rim_list[0], rim_list[1], rim_list[2], rim_list[3], rim_list[4]), "grp", 1)
    filtered = []
    for rate_level in range(len(levels)):
        result_level = filter_level(
            history[rate_level], levels[rate_level], basis_bf, 2**rate_level
        )
        filtered.append(result_level.astype(jnp.bfloat16)[None])
    return (mixing, spectrum, filtered[0], filtered[1], filtered[2], filtered[3], filtered[4])


def solution(mesh):
    return jax.shard_map(
        local,
        mesh=mesh,
        in_specs=(
            P(("bin", "grp"), None),
            P(("bin", "grp"), None),
            P(("bin", "grp")),
            P(),
            P(),
            P(None, "grp"),
        ),
        out_specs=(
            P(("bin", "grp"), None),
            P("bin", None),
            P("bin", None, "grp", None),
            P("bin", None, "grp", None),
            P("bin", None, "grp", None),
            P("bin", None, "grp", None),
            P("bin", None, "grp", None),
        ),
        check_vma=False,
    )
```

profile of v0, /device:TPU:0, one launch (start us, length us, event | category | flops | bytes accessed | tf_op | source)
XLA Modules:
  0.0 447.3 jit_solution(9783774294993222172)
XLA Ops:
  7.9 9.0 %reduce-window.6 = s32[32,8,128]{2,1,0:T(8,128)S(1)} reduce-window(s32[32,8,128]{2,1,0:T(8,128)S(1)} %fusion.30, s32[]{:T(128)} %copy.52), window={size=1x1x128 pad=0_0x0_0x127_0}, to_apply=%region_0.1 | reduce-window | flops 4161536 | bytes 262148 | tf_op jit(solution)/shard_map/reduce-window
  18.9 0.9 fusion.52
  20.5 7.8 %scatter_custom_fusion = bf16[2048,512]{1,0:T(8,128)(2,1)} fusion(s32[1024]{0:T(1024)S(1)} %bitcast.151, bf16[1024,512]{1,0:T(8,128)(2,1)} %param.6, f32[512]{0:T(512)S(1)} %bitcast.157, f32[512]{0:T(512)S(1)} %bitcast.158, f32[512]{0:T(512)S(1)} %bitcast.155, f32[512]{0:T(512)S(1)} %bitcast.156, f32[]{:T(128)} %constant.105.clone.1, f32[512]{0:T(512)S(1)} %bitcast.154, ...), kind=kCustom, calls=%fused_computation.26 | custom fusion | flops 6291456 | bytes 3161094 | tf_op jit(solution)/shard_map/scatter | solution.py:75
  28.3 7.4 %all-to-all-start = ((bf16[32,64,512]{2,1,0:T(8,128)(2,1)}), bf16[32,64,512]{2,1,0:T(8,128)(2,1)}, u32[]{:S(2)}, u32[]{:S(2)}) async-start(bf16[32,64,512]{2,1,0:T(8,128)(2,1)} %bitcast.11), calls=%async_computation | async-start | bytes 4194304 | tf_op jit(solution)/shard_map/all_to_all | solution.py:76
  35.8 2.1 collective-permute-start
  37.9 6.4 %reshape.114 = f32[2,4096,2]{2,1,0:T(8,128)} reshape(f32[2,8192]{1,0:T(2,128)S(1)} %copy-done.5) | data formatting | bytes 131072 | tf_op jit(solution)/shard_map/reshape | solution.py:32
  44.4 5.9 %convert_reduce_fusion = bf16[2,4096]{1,0:T(2,128)(2,1)S(1)} fusion(f32[2,4096,2]{2,1,0:T(8,128)} %reshape.114), kind=kLoop, calls=%fused_computation.17 | loop fusion | flops 24576 | bytes 81920 | tf_op jit(solution)/shard_map/convert_element_type | solution.py:34
  50.3 4.0 collective-permute-start.1
  54.3 2.4 fusion.3
  56.6 2.2 mul.59
  58.8 1.2 convert_reduce_fusion.1
  60.0 2.1 collective-permute-start.2
  62.1 1.2 fusion.18
  63.3 1.0 mul.62
  65.1 3.3 collective-permute-start.3
  70.0 2.0 collective-permute-start.4
  76.7 1.1 copy.27
  77.9 7.9 %all-to-all-done = bf16[32,64,512]{2,1,0:T(8,128)(2,1)} async-done(((bf16[32,64,512]{2,1,0:T(8,128)(2,1)}), bf16[32,64,512]{2,1,0:T(8,128)(2,1)}, u32[]{:S(2)}, u32[]{:S(2)}) %all-to-all-start) | async-done | bytes 2097184 | tf_op jit(solution)/shard_map/all_to_all | solution.py:76
  85.8 4.5 convolution_bitcast_fusion
  90.6 1.4 copy.24
  92.1 59.0 %all-reduce.3.cloned.1.call-done = f32[512,512]{1,0:T(8,128)} async-done(((f32[512,512]{1,0:T(8,128)}), f32[512,512]{1,0:T(8,128)}) %all-reduce.3.cloned.1.call-update) | async-done | bytes 1048592 | tf_op jit(solution)/shard_map/psum | solution.py:80
  151.1 2.2 fusion.54
  153.3 1.0 fusion.55
  154.6 11.7 %cholesky.50 = f32[128,128]{1,0:T(8,128)S(1)} custom-call(f32[128,128]{1,0:T(8,128)S(1)} %cholesky.118), custom_call_target="Cholesky" | custom-call | tf_op jit(solution)/shard_map/jit(cholesky)/cholesky | solution.py:53
  166.3 9.8 %custom-call.15 = f32[1,128,128]{1,2,0:T(8,128)S(1)} custom-call(f32[1,128,128]{2,1,0:T(8,128)S(1)} %get-tuple-element.30), custom_call_target="InvertDiagBlocksLowerTriangular" | custom-call | tf_op jit(solution)/shard_map/jit(cholesky)/cholesky | solution.py:53
  176.6 12.1 %cholesky.105 = f32[128,128]{1,0:T(8,128)S(1)} custom-call(f32[128,128]{1,0:T(8,128)S(1)} %convolution_subtract_fusion.1), custom_call_target="Cholesky" | custom-call | tf_op jit(solution)/shard_map/jit(cholesky)/cholesky | solution.py:53
  190.8 4.0 while.1
  191.4 1.4 bitcast_dynamic-update-slice_fusion.2
  193.4 1.4 bitcast_dynamic-update-slice_fusion.2
  194.8 19.7 %custom-call.16 = f32[2,128,128]{1,2,0:T(8,128)S(1)} custom-call(f32[2,128,128]{2,1,0:T(8,128)S(1)} %get-tuple-element.14), custom_call_target="InvertDiagBlocksLowerTriangular" | custom-call | tf_op jit(solution)/shard_map/jit(_solve_triangular)/triangular_solve | solution.py:54
  216.8 6.6 %slice.147 = bf16[256,256]{0,1:T(8,128)(2,1)} slice(bf16[512,256]{0,1:T(8,128)(2,1)S(1)} %fusion.27), slice={[0:512:2], [0:256:1]} | slice | bytes 262144 | tf_op jit(solution)/shard_map/slice | solution.py:39
  223.5 3.0 slice.152
  226.4 1.9 slice.157
  228.3 1.3 slice.162
  229.6 3.3 convolution_convert_fusion
  232.9 3.7 all-to-all-start.1
  236.6 2.3 gather_fusion.1
  240.0 123.6 %select_convert_fusion = bf16[16,1088,256]{2,0,1:T(8,128)(2,1)} fusion(pred[16,1088]{0,1:T(8,128)(4,1)S(1)} %bitcast.160, bf16[16,1599,1]{0,2,1:T(2,128)(2,1)S(1)} %copy.24, bf16[512,1,256]{2,1,0:T(2,128)(2,1)S(1)} %copy.25), kind=kOutput, calls=%fused_computation.5 | convolution fusion | flops 4572315648 | bytes 9243616 | tf_op jit(solution)/shard_map/conv_general_dilated | solution.py:41
  363.6 10.2 %copy.26 = bf16[16,1088,256]{2,1,0:T(8,128)(2,1)} copy(bf16[16,1088,256]{2,0,1:T(8,128)(2,1)} %select_convert_fusion) | data formatting | bytes 17825792 | tf_op jit(solution)/shard_map/convert_element_type | solution.py:97
  374.4 31.3 %select_convert_fusion.1 = bf16[16,544,256]{2,0,1:T(8,128)(2,1)S(1)} fusion(pred[16,544]{0,1:T(8,128)(4,1)S(1)} %bitcast.161, bf16[16,799,1]{0,2,1:T(2,128)(2,1)S(1)} %copy-done.4, bf16[256,1,256]{2,1,0:T(2,128)(2,1)S(1)} %copy.28), kind=kOutput, calls=%fused_computation.6 | convolution fusion | flops 1145307136 | bytes 4621792 | tf_op jit(solution)/shard_map/conv_general_dilated | solution.py:41
  405.7 1.6 copy.29
  407.3 2.3 slice_bitcast_fusion.1
  410.0 8.4 %select_convert_fusion.2 = bf16[16,272,256]{2,0,1:T(8,128)(2,1)S(1)} fusion(pred[16,272]{0,1:T(8,128)(4,1)S(1)} %copy-done.15, bf16[16,399,1]{0,2,1:T(2,128)(2,1)S(1)} %copy-done.9, bf16[128,1,256]{2,1,0:T(2,128)(2,1)S(1)} %copy.31), kind=kOutput, calls=%fused_computation.8 | convolution fusion | flops 287440896 | bytes 2310880 | tf_op jit(solution)/shard_map/conv_general_dilated | solution.py:41
  419.1 1.5 slice_bitcast_fusion.2
  420.9 2.5 select_convert_fusion.3
  423.8 1.0 slice_bitcast_fusion.3
  426.9 7.3 %slice_bitcast_fusion = bf16[1,2,8192,256]{3,2,1,0:T(8,128)(2,1)} fusion(bf16[2,8704,256]{2,1,0:T(8,128)(2,1)} %bitcast.135), kind=kLoop, calls=%fused_computation.7 | loop fusion | bytes 16777216 | tf_op jit(solution)/shard_map/broadcast_in_dim | solution.py:97
  434.3 6.0 %gather_fusion = bf16[1024,256]{1,0:T(8,128)(2,1)} fusion(bf16[2048,256]{1,0:T(8,128)(2,1)} %bitcast.21, s32[1024]{0:T(1024)S(1)} %copy-done.12), kind=kCustom, calls=%fused_computation | custom fusion | bytes 1052672 | tf_op jit(solution)/shard_map/gather | solution.py:85
  (138 shorter events, 21.2 us)
Async XLA Ops:
  7.2 143.9 %copy-start = (f32[512,256]{1,0:T(8,128)S(1)}, f32[512,256]{1,0:T(8,128)}, u32[]{:S(2)}) copy-start(f32[512,256]{1,0:T(8,128)} %param.10) | copy-start | bytes 1572868
  28.3 7.5 %copy-start.5 = (f32[2,8192]{1,0:T(2,128)S(1)}, f32[2,8192]{1,0:T(2,128)}, u32[]{:S(2)}) copy-start(f32[2,8192]{1,0:T(2,128)} %param.11) | copy-start | bytes 196612
  28.3 57.5 %all-to-all-start = ((bf16[32,64,512]{2,1,0:T(8,128)(2,1)}), bf16[32,64,512]{2,1,0:T(8,128)(2,1)}, u32[]{:S(2)}, u32[]{:S(2)}) async-start(bf16[32,64,512]{2,1,0:T(8,128)(2,1)} %bitcast.11), calls=%async_computation | async-start | bytes 4194304 | tf_op jit(solution)/shard_map/all_to_all | solution.py:76
  35.7 115.4 %all-reduce.3.cloned.1.call-start = ((), (), s32[]{:S(2)}) async-start(), calls=%async_computation.2 | async-start | bytes 2097152 | tf_op jit(solution)/shard_map/psum | solution.py:80
  35.8 42.0 %collective-permute-start = (bf16[2,512]{1,0:T(2,128)(2,1)S(1)}, bf16[2,512]{1,0:T(2,128)(2,1)S(1)}, u32[]{:S(2)}, u32[]{:S(2)}) collective-permute-start(bf16[2,512]{1,0:T(2,128)(2,1)S(1)} %slice.190), channel_id=1, source_target_pairs={{0,1},{1,2},{2,3},{3,4},{4,5},{5,6},{6,7},{8,9},{9,10},{10,11},{11... | collective-permute-start | bytes 6152 | tf_op jit(solution)/shard_map/ppermute | solution.py:15
  44.4 9.9 %copy-start.2 = (f32[2,4096,2]{2,1,0:T(8,128)S(1)}, f32[2,4096,2]{2,1,0:T(8,128)}, u32[]{:S(2)}) copy-start(f32[2,4096,2]{2,1,0:T(8,128)} %reshape.114) | copy-start | bytes 196612
  50.3 26.1 %collective-permute-start.1 = (bf16[2,256]{1,0:T(2,128)(2,1)S(1)}, bf16[2,256]{1,0:T(2,128)(2,1)S(1)}, u32[]{:S(2)}, u32[]{:S(2)}) collective-permute-start(bf16[2,256]{1,0:T(2,128)(2,1)S(1)} %slice.196), channel_id=1, source_target_pairs={{0,1},{1,2},{2,3},{3,4},{4,5},{5,6},{6,7},{8,9},{9,10},{10,11},{11... | collective-permute-start | bytes 3080 | tf_op jit(solution)/shard_map/ppermute | solution.py:15
  60.0 15.1 %collective-permute-start.2 = (bf16[2,128]{1,0:T(2,128)(2,1)S(1)}, bf16[2,128]{1,0:T(2,128)(2,1)S(1)}, u32[]{:S(2)}, u32[]{:S(2)}) collective-permute-start(bf16[2,128]{1,0:T(2,128)(2,1)S(1)} %slice.202), channel_id=1, source_target_pairs={{0,1},{1,2},{2,3},{3,4},{4,5},{5,6},{6,7},{8,9},{9,10},{10,11},{11... | collective-permute-start | bytes 1544 | tf_op jit(solution)/shard_map/ppermute | solution.py:15
  65.1 8.9 %collective-permute-start.3 = (bf16[2,64]{1,0:T(2,128)(2,1)S(1)}, bf16[2,64]{1,0:T(2,128)(2,1)S(1)}, u32[]{:S(2)}, u32[]{:S(2)}) collective-permute-start(bf16[2,64]{1,0:T(2,128)(2,1)S(1)} %slice.207), channel_id=1, source_target_pairs={{0,1},{1,2},{2,3},{3,4},{4,5},{5,6},{6,7},{8,9},{9,10},{10,11},{11... | collective-permute-start | bytes 776 | tf_op jit(solution)/shard_map/ppermute | solution.py:15
  70.0 2.9 collective-permute-start.4
  232.9 7.0 %copy-start.13 = (pred[16,1088]{0,1:T(32,128)(4,1)S(1)}, pred[16,1088]{0,1:T(32,128)(4,1)}, u32[]{:S(2)}) copy-start(pred[16,1088]{0,1:T(32,128)(4,1)} %constant.152) | copy-start | bytes 52228
  232.9 201.3 %all-to-all-start.1 = ((bf16[32,64,256]{2,1,0:T(8,128)(2,1)}), bf16[32,64,256]{2,1,0:T(8,128)(2,1)}, u32[]{:S(2)}, u32[]{:S(2)}) async-start(bf16[32,64,256]{2,1,0:T(8,128)(2,1)} %bitcast.20), calls=%async_computation.1 | async-start | bytes 2097152 | tf_op jit(solution)/shard_map/all_to_all | solution.py:84
  363.5 10.3 %copy-start.3 = (bf16[256,256]{0,1:T(8,128)(2,1)S(1)}, bf16[256,256]{0,1:T(8,128)(2,1)}, u32[]{:S(2)}) copy-start(bf16[256,256]{0,1:T(8,128)(2,1)} %slice.147) | copy-start | bytes 393220
  363.6 10.9 %copy-start.4 = (bf16[16,799,1]{0,2,1:T(2,128)(2,1)S(1)}, bf16[16,799,1]{0,2,1:T(2,128)(2,1)}, u32[]{:S(2)}) copy-start(bf16[16,799,1]{0,2,1:T(2,128)(2,1)} %copy.27) | copy-start | bytes 76708
  363.6 10.9 %copy-start.14 = (pred[16,544]{0,1:T(32,128)(4,1)S(1)}, pred[16,544]{0,1:T(32,128)(4,1)}, u32[]{:S(2)}) copy-start(pred[16,544]{0,1:T(32,128)(4,1)} %constant.153) | copy-start | bytes 26116
  407.3 2.3 copy-start.8
  407.3 2.7 copy-start.9
  407.3 2.7 copy-start.15
  419.1 1.5 copy-start.7
  419.1 1.8 copy-start.10
  419.1 1.8 copy-start.16
  423.4 1.4 copy-start.6
  423.4 1.7 copy-start.11
  423.4 1.7 copy-start.17
  426.9 7.3 %copy-start.12 = (s32[1024]{0:T(1024)S(1)}, s32[1024]{0:T(1024)}, u32[]{:S(2)}) copy-start(s32[1024]{0:T(1024)} %broadcast_clamp_fusion) | copy-start | bytes 12292
  434.3 6.0 %copy-start.1 = (f32[512,256]{1,0:T(8,128)S(1)}, f32[512,256]{1,0:T(8,128)}, u32[]{:S(2)}) copy-start(f32[512,256]{1,0:T(8,128)} %param.10) | copy-start | bytes 1572868
Sparse Core Ops, SparseCore 0:
  90.4 60.6 all-reduce.2
where the time goes:
time: 455 us; the launch traced here: 447 us
  matrix products  179 us (39%)
  other arithmetic  88.3 us (19%)
  local copies, waits for them, and re-layouts  71.7 us (16%)
  waiting for transfers between devices  67.2 us (15%)
  starting transfers between devices  24.7 us (5%)
  between operations  16.3 us (4%)
    conv_general_dilated x5, matrix products, filter_level(): lax.conv_general_dilated(joined[:, :, None], tap_rows[::-1][:, None, :],...  166 us
    psum x1, waiting for transfers between devices, local(): gram_total = lax.psum(partial_gram, 'grp')  59 us
    another operation x6, other arithmetic, basis_from(): lower_factor = jnp.linalg.cholesky(inner_gram)  34.3 us
    another operation x3, other arithmetic, basis_from(): jax.scipy.linalg.solve_triangular(lower_factor, product.T, lower=True)  19.7 us
    ppermute x5, starting transfers between devices, shifted(): return lax.ppermute(x, axis, pairs)  13.5 us
    convert_element_type x6, local copies, waits for them, and re-layouts, local(): filtered.append(result_level.astype(jnp.bfloat16)[None])  13.2 us
    broadcast_in_dim x5, local copies, waits for them, and re-layouts, local(): filtered.append(result_level.astype(jnp.bfloat16)[None])  12.9 us
    slice x4, local copies, waits for them, and re-layouts, filter_level(): tap_rows = basis_bf[::stride]  12.8 us
  transfers between devices with their start and end apart: 8, of which 3 were waited for; matrix products, arithmetic and copies ran while one was open for 51% of the time, Pallas kernels for 0%

commit v1 on v0

v1 whole, which is shorter than its diff:
```python
import functools
import math

import jax
import jax.numpy as jnp
from jax import lax
from jax.experimental import pallas as pl
from jax.experimental.pallas import tpu as pltpu
from jax.sharding import PartitionSpec as P

highest = lax.Precision.HIGHEST
inv_root_two = 0.7071067811865476
f32 = jnp.float32
bf16 = jnp.bfloat16
LANES = 128
BLOCK = 32
VMEM_BYTES = 60 * 1024 * 1024


def iota(shape, axis):
    return lax.broadcasted_iota(jnp.int32, shape, axis)


def split3(x):
    high = x.astype(bf16)
    rest = x - high.astype(f32)
    middle = rest.astype(bf16)
    low = (rest - middle.astype(f32)).astype(bf16)
    return high, middle, low


def dot(a, b, precision=None):
    return jnp.dot(a, b, preferred_element_type=f32, precision=precision)


def dot_t(a, b, precision=None):
    return lax.dot_general(
        a, b, (((0,), (0,)), ((), ())), preferred_element_type=f32, precision=precision
    )


def params(**kw):
    return pltpu.CompilerParams(vmem_limit_bytes=VMEM_BYTES, **kw)


def spread(group, rows, groups, width):
    member = (iota((8, rows), 0) == group).astype(f32).astype(bf16)
    column = (iota((8, groups * width), 0) == iota((8, groups * width), 1) // width).astype(f32)
    return dot_t(member, column.astype(bf16))


def front_body(bins, grp, place_ref, owner_ref, code_ref, gains_ref, templates_ref, sketch_ref,
               white_ref, keep_ref, send_ref, product_ref):
    rows, width = templates_ref.shape
    rank = sketch_ref.shape[1]
    rates = gains_ref.shape[0]
    gains = jnp.concatenate([gains_ref[...], jnp.zeros((8 - rates, width), f32)], axis=0)
    member = (iota((8, rows), 0) == code_ref[...]).astype(f32)
    member = jnp.concatenate([member, member, member], axis=0).astype(bf16)
    parts = jnp.concatenate([part.astype(f32) for part in split3(gains)], axis=0).astype(bf16)
    factor = dot_t(member, parts)
    white = (templates_ref[...].astype(f32) * factor).astype(bf16)
    white_ref[...] = white
    sketched = None
    for part in split3(sketch_ref[...]):
        term = dot(white, part)
        sketched = term if sketched is None else sketched + term
    mask = spread(owner_ref[...] // grp, rows, bins, rank).astype(bf16)
    total = None
    for part in split3(sketched):
        term = dot_t(white, jnp.concatenate([part] * bins, axis=1) * mask)
        total = term if total is None else total + term
    product_ref[...] = total
    half = width // 2
    core = place_ref[0]
    for b in range(bins):
        columns = slice(b * rank, (b + 1) * rank)
        keep_ref[b] = product_ref[pl.ds(pl.multiple_of(core * half, half), half), columns]
        send_ref[b] = product_ref[pl.ds(pl.multiple_of((1 - core) * half, half), half), columns]


def front(place, owner, code, gains, templates, sketch, bins, grp):
    rows, width = templates.shape
    rank = sketch.shape[1]
    half = jax.ShapeDtypeStruct((bins, width // 2, rank), f32)
    vmem = pl.BlockSpec(memory_space=pltpu.VMEM)
    return pl.pallas_call(
        functools.partial(front_body, bins, grp),
        out_shape=(jax.ShapeDtypeStruct((rows, width), bf16), half, half),
        in_specs=[pl.BlockSpec(memory_space=pltpu.SMEM)] + [vmem] * 5,
        out_specs=(vmem, vmem, vmem),
        scratch_shapes=[pltpu.VMEM((width, bins * rank), f32)],
        compiler_params=params(),
        name="whiten_product",
    )(place, owner, code, gains, templates, sketch)


def pick(x, index):
    return lax.dynamic_index_in_dim(x, index, 0, keepdims=False)


def flip_bin(x, bit, bins):
    return lax.ppermute(x, "bin", [(i, i ^ bit) for i in range(bins)])


def flip_grp(x, bit, grp):
    return lax.ppermute(x, "grp", [(i, i ^ bit) for i in range(grp)])


def reduce_products(keep, send, bins, grp):
    total = keep + flip_grp(send, 1, grp)
    rows = total.shape[1]
    here = lax.axis_index("bin")
    high, low = here >> 1, here & 1

    def by(x, bit):
        x = x.reshape((2, 2) + x.shape[1:])
        return x if bit else jnp.swapaxes(x, 0, 1)

    first = by(total[:, : rows // 2], 0)
    second = by(total[:, rows // 2 :], 1)
    first = pick(first, low) + flip_bin(pick(first, 1 - low), 1, bins)
    second = pick(second, high) + flip_bin(pick(second, 1 - high), 2, bins)
    first = pick(first, high) + flip_bin(pick(first, 1 - high), 2, bins)
    second = pick(second, low) + flip_bin(pick(second, 1 - low), 1, bins)
    mine = jnp.concatenate([first, second], axis=0)
    chips = grp // 2
    chip = lax.axis_index("grp") // 2
    shares = mine.reshape((chips, rows // chips) + mine.shape[1:])
    share = pick(shares, chip)
    for d in range(1, chips):
        share = share + flip_grp(pick(shares, chip ^ d), 2 * d, grp)
    pieces = jnp.stack([share] + [flip_grp(share, 2 * d, grp) for d in range(1, chips)])
    other = flip_grp(pieces, 1, grp)
    return pieces, other


def basis_body(place_ref, mine_ref, other_ref, taps_ref, diag_ref, product_ref, work_ref, wide_ref):
    chips, share, rank = mine_ref.shape
    length = 2 * chips * share
    half = length // 2
    core, chip = place_ref[0], place_ref[1]
    for d in range(chips):
        row = (chip ^ d) * share
        product_ref[pl.ds(pl.multiple_of(core * half + row, share), share), :] = mine_ref[d]
        product_ref[pl.ds(pl.multiple_of((1 - core) * half + row, share), share), :] = other_ref[d]
    product = product_ref[...]
    product_t = product.T
    work_ref[:, :rank] = dot(product_t, product, highest)
    work_ref[:, rank:] = product_t
    lane = iota((BLOCK, LANES), 1)
    row_at = iota((BLOCK, LANES), 0)
    per_tile = LANES // BLOCK
    for j in range(rank // BLOCK):
        rows = slice(j * BLOCK, (j + 1) * BLOCK)
        offset = (j % per_tile) * BLOCK
        eye_at = ((j + 1) % per_tile) * BLOCK
        tile_at = (j // per_tile) * LANES
        tile = work_ref[rows, tile_at : tile_at + LANES]
        state = jnp.where(
            (lane >= offset) & (lane < offset + BLOCK),
            tile,
            jnp.where(lane == row_at + eye_at, f32(1.0), f32(0.0)),
        )
        for k in range(BLOCK):
            column = jnp.broadcast_to(state[:, offset + k : offset + k + 1], (BLOCK, LANES))
            scale = 1.0 / column[k : k + 1, :]
            state = state - jnp.where(row_at > k, column, f32(0.0)) * (state[k : k + 1, :] * scale)
        pivot = jnp.sum(jnp.where(lane == row_at + offset, state, f32(0.0)), axis=1, keepdims=True)
        inverse = state[:, eye_at : eye_at + BLOCK] * lax.rsqrt(pivot)
        solved = dot(inverse, work_ref[rows, :], highest)
        work_ref[rows, :] = solved
        after = (j + 1) * BLOCK
        if after < rank:
            change = dot_t(solved[:, :rank], solved, highest)
            work_ref[after:, :] = work_ref[after:, :] - change[after:, :]
    on_diagonal = iota((rank, rank), 0) == iota((rank, rank), 1)
    diag_ref[...] = jnp.sum(
        jnp.where(on_diagonal, work_ref[:, :rank], f32(0.0)), axis=0, keepdims=True
    )
    basis = work_ref[:, rank:].T
    for part in range(rank // LANES):
        wide_ref[part] = basis[:, part * LANES : (part + 1) * LANES]
    at = 0
    taps, level = length, 0
    while at < taps_ref.shape[0]:
        rows = max(taps, LANES)
        chosen = jnp.concatenate(
            [wide_ref[part, pl.ds(0, taps, stride=2**level), :] for part in range(rank // LANES)],
            axis=1,
        )
        if rows > taps:
            chosen = jnp.concatenate([chosen, jnp.zeros((rows - taps, rank), f32)], axis=0)
        taps_ref[at : at + rows, :] = chosen.astype(bf16)
        at, taps, level = at + rows, taps // 2, level + 1


def find_basis(place, mine, other, tap_rows):
    chips, share, rank = mine.shape
    length = 2 * chips * share
    vmem = pl.BlockSpec(memory_space=pltpu.VMEM)
    return pl.pallas_call(
        basis_body,
        out_shape=(
            jax.ShapeDtypeStruct((tap_rows, rank), bf16),
            jax.ShapeDtypeStruct((1, rank), f32),
        ),
        in_specs=[pl.BlockSpec(memory_space=pltpu.SMEM), vmem, vmem],
        out_specs=(vmem, vmem),
        scratch_shapes=[
            pltpu.VMEM((length, rank), f32),
            pltpu.VMEM((rank, rank + length), f32),
            pltpu.VMEM((rank // LANES, length, LANES), f32),
        ],
        compiler_params=params(),
        name="cholesky_basis",
    )(place, mine, other)


def level_sizes(levels, tap_count):
    return [max(1, (tap_count >> r) // LANES) for r in range(levels)]


def tiles_body(levels, blocks, detectors, chunks, strain_ref, tiles_ref, level_ref, flipped_ref):
    step = pl.program_id(0)
    total = strain_ref.shape[0]
    starts = [0]
    for r in range(levels):
        starts.append(starts[-1] + (total >> r))

    @pl.when(step == 0)
    def _():
        source = iota((2 * LANES, 2 * LANES), 0)
        target = iota((2 * LANES, 2 * LANES), 1)
        even_odd = (source == 2 * (target % LANES) + target // LANES).astype(f32).astype(bf16)
        reverse = (
            iota((LANES, LANES), 0) + iota((LANES, LANES), 1) == LANES - 1
        ).astype(f32).astype(bf16)
        level_ref[: total, :] = strain_ref[...]
        for r in range(levels):
            rows = total >> r
            at = starts[r]
            if r > 0:
                before = starts[r - 1]
                joined = jnp.concatenate(
                    [
                        level_ref[pl.ds(before, rows, stride=2), :],
                        level_ref[pl.ds(before + 1, rows, stride=2), :],
                    ],
                    axis=1,
                )
                high, middle, low = split3(joined)
                both = (dot(high, even_odd) + dot(middle, even_odd)) + dot(low, even_odd)
                level_ref[at : at + rows, :] = (both[:, :LANES] + both[:, LANES:]) * inv_root_two
            flipped_ref[at : at + rows, :] = dot(level_ref[at : at + rows, :].astype(bf16), reverse)

    detector = step // chunks
    chunk = step % chunks
    lower = iota((LANES, LANES), 1) <= iota((LANES, LANES), 0)
    at = 0
    for r in range(levels):
        rows = (total >> r) // detectors
        history = (1 << (levels - 1)) >> r
        count = (rows - history) // chunks
        first = starts[r] + detector * rows + history + chunk * count - (blocks[r] - 1)

        def turned(row):
            line = jnp.broadcast_to(flipped_ref[pl.ds(row, 1), :], (LANES, LANES))
            return pltpu.roll(line, 1, 1, stride=1, stride_axis=0)

        before = turned(first - 1)
        for i in range(count + blocks[r] - 1):
            now = turned(first + i)
            tiles_ref[0, at] = jnp.where(lower, now, before).astype(bf16)
            before = now
            at += 1


def make_tiles(strain_rows, levels, blocks, detectors, chunks):
    total = strain_rows.shape[0]
    count = 0
    for r in range(levels):
        rows = (total >> r) // detectors
        history = (1 << (levels - 1)) >> r
        count += (rows - history) // chunks + blocks[r] - 1
    steps = detectors * chunks
    held = sum(total >> r for r in range(levels))
    held = -(-held // 8) * 8
    return pl.pallas_call(
        functools.partial(tiles_body, levels, blocks, detectors, chunks),
        grid=(steps,),
        out_shape=jax.ShapeDtypeStruct((steps, count, LANES, LANES), bf16),
        in_specs=[pl.BlockSpec((total, LANES), lambda i: (0, 0))],
        out_specs=pl.BlockSpec((1, count, LANES, LANES), lambda i: (i, 0, 0, 0)),
        scratch_shapes=[pltpu.VMEM((held, LANES), f32), pltpu.VMEM((held, LANES), f32)],
        compiler_params=params(),
        cost_estimate=pl.CostEstimate(
            flops=steps * count * LANES * LANES * 64, bytes_accessed=steps * count * LANES * LANES * 2,
            transcendentals=0,
        ),
        name="toeplitz_tiles",
    )(strain_rows)


def filter_body(blocks, tiles_ref, taps_ref, *out_refs):
    at, tap_at = 0, 0
    for r, out_ref in enumerate(out_refs):
        count = out_ref.shape[2] // LANES
        b = blocks[r]
        taps = taps_ref[tap_at : tap_at + b * LANES, :]
        group = min(count, 4)
        for i in range(0, count, group):
            columns = [
                tiles_ref[0, at + b - 1 - k + i : at + b - 1 - k + i + group].reshape(
                    group * LANES, LANES
                )
                for k in range(b)
            ]
            joined = jnp.concatenate(columns, axis=1) if b > 1 else columns[0]
            out_ref[0, 0, i * LANES : (i + group) * LANES, :] = dot(joined, taps).astype(bf16)
        at += count + b - 1
        tap_at += b * LANES


def filter_levels(tiles, taps, lengths, blocks, detectors, chunks):
    rank = taps.shape[1]
    steps, count = tiles.shape[:2]
    out_shape = [jax.ShapeDtypeStruct((1, detectors, n, rank), bf16) for n in lengths]
    return pl.pallas_call(
        functools.partial(filter_body, blocks),
        grid=(steps,),
        out_shape=out_shape,
        in_specs=[
            pl.BlockSpec((1, count, LANES, LANES), lambda i: (i, 0, 0, 0)),
            pl.BlockSpec(taps.shape, lambda i: (0, 0)),
        ],
        out_specs=[
            pl.BlockSpec((1, 1, n // chunks, rank), lambda i: (0, i // chunks, i % chunks, 0))
            for n in lengths
        ],
        compiler_params=params(),
        cost_estimate=pl.CostEstimate(
            flops=8 * sum(lengths) * LANES * rank * detectors,
            bytes_accessed=2 * detectors * sum(lengths) * rank + 2 * math.prod(tiles.shape),
            transcendentals=0,
        ),
        name="filter_levels",
    )(tiles, taps)


def mixing_body(bins, grp, place_ref, owner_ref, white_ref, own_ref, mine_ref, other_ref, out_ref,
                bases_ref):
    rows, width = white_ref.shape
    rank = own_ref.shape[1]
    half = width // 2
    core, here = place_ref[0], place_ref[2]
    bases_ref[0] = own_ref[...]
    for m in range(1, bins):
        bases_ref[m, pl.ds(pl.multiple_of(core * half, half), half), :] = mine_ref[m - 1]
        bases_ref[m, pl.ds(pl.multiple_of((1 - core) * half, half), half), :] = other_ref[m - 1]
    mask = spread((owner_ref[...] // grp) ^ here, rows, bins, rank)
    white = white_ref[...]
    total = None
    for m in range(bins):
        chosen = mask[:, m * rank : (m + 1) * rank] > 0.5
        term = jnp.where(chosen, dot(white, bases_ref[m]), f32(0.0))
        total = term if total is None else total + term
    out_ref[...] = total.astype(bf16)


def mix(place, owner, white, own, mine, other, grp):
    rows, width = white.shape
    rank = own.shape[1]
    bins = mine.shape[0] + 1
    vmem = pl.BlockSpec(memory_space=pltpu.VMEM)
    return pl.pallas_call(
        functools.partial(mixing_body, bins, grp),
        out_shape=jax.ShapeDtypeStruct((rows, rank), bf16),
        in_specs=[pl.BlockSpec(memory_space=pltpu.SMEM)] + [vmem] * 5,
        out_specs=vmem,
        scratch_shapes=[pltpu.VMEM((bins, width, rank), bf16)],
        compiler_params=params(),
        name="mixing",
    )(place, owner, white, own, mine, other)


def local(templates, owner_device, rate_code, rate_gains, sketch, strain):
    rows, width = templates.shape
    grp = lax.axis_size("grp")
    bins = lax.axis_size("bin")
    levels = rate_gains.shape[0]
    detectors, samples = strain.shape
    here, spot = lax.axis_index("bin"), lax.axis_index("grp")
    place = jnp.stack([spot % 2, spot // 2, here]).astype(jnp.int32)
    owner = owner_device.reshape(1, rows)

    white, keep, send = front(
        place, owner, rate_code.reshape(1, rows), rate_gains, templates, sketch, bins, grp
    )

    reach = LANES << (levels - 1)
    history = lax.ppermute(strain[:, -reach:], "grp", [(i, i + 1) for i in range(grp - 1)])
    strain_rows = jnp.concatenate([history, strain], axis=1).reshape(-1, LANES)
    blocks = level_sizes(levels, width)
    chunks = 4
    tiles = make_tiles(strain_rows, levels, blocks, detectors, chunks)

    mine, other = reduce_products(keep, send, bins, grp)
    taps, diag = find_basis(place, mine, other, sum(blocks) * LANES)
    own = taps[:width]
    part = lax.dynamic_slice_in_dim(own, (spot % 2) * (width // 2), width // 2, 0)
    theirs = jnp.stack([flip_bin(part, m, bins) for m in range(1, bins)])
    theirs_other = flip_grp(theirs, 1, grp)
    lengths = [samples >> r for r in range(levels)]
    filtered = filter_levels(tiles, taps, lengths, blocks, detectors, chunks)
    mixing = mix(place, owner, white, own, theirs, theirs_other, grp)
    spectrum = diag / (rows * grp * math.sqrt(width))
    return (mixing, spectrum, *filtered)


def solution(mesh):
    return jax.shard_map(
        local,
        mesh=mesh,
        in_specs=(
            P(("bin", "grp"), None),
            P(("bin", "grp"), None),
            P(("bin", "grp")),
            P(),
            P(),
            P(None, "grp"),
        ),
        out_specs=(
            P(("bin", "grp"), None),
            P("bin", None),
            P("bin", None, "grp", None),
            P("bin", None, "grp", None),
            P("bin", None, "grp", None),
            P("bin", None, "grp", None),
            P("bin", None, "grp", None),
        ),
        check_vma=False,
    )
```

time: 455 us -> 115 us (0.25); the launches traced: 447 us -> 115 us
  matrix products: 179 us -> 0 us
  other arithmetic: 88.3 us -> 2.77 us
  local copies, waits for them, and re-layouts: 71.7 us -> 3.35 us
  Pallas kernels: 0 us -> 64.1 us
  waiting for transfers between devices: 67.2 us -> 20.3 us
  between operations: 16.3 us -> 0.9 us
    conv_general_dilated x5 -> x0, matrix products: 166 us -> none  [filter_level(): lax.conv_general_dilated(joined[:, :, None], tap_rows[::-1][:, None, :],...]
    pallas_call x0 -> x5, Pallas kernels: none -> 64.1 us  [the longest x1 30.2 us: find_basis(): pl.pallas_call(basis_body, out_shape=(jax.ShapeDtypeStruct((tap_rows, ran...]
    another operation x12 -> x3, other arithmetic: 63.2 us -> 0.67 us  [the longest x1 0.6 us: local(): place = jnp.stack([spot % 2, spot // 2, here]).astype(jnp.int32)]
    psum x1 -> x0, waiting for transfers between devices: 59 us -> none  [local(): gram_total = lax.psum(partial_gram, 'grp')]
    ppermute x5 -> x17, waiting for transfers between devices: 0.2 us -> 20.3 us  [the longest x9 11.8 us: flip_grp(): return lax.ppermute(x, 'grp', [(i, i ^ bit) for i in range(grp)])]
    broadcast_in_dim x15 -> x0, local copies, waits for them, and re-layouts: 14 us -> none  [the longest x5 12.9 us: local(): filtered.append(result_level.astype(jnp.bfloat16)[None])]
    slice x15 -> x3, local copies, waits for them, and re-layouts: 14.2 us -> 1.04 us  [the longest x1 0.97 us: local(): own = taps[:width]]
    convert_element_type x6 -> x0, local copies, waits for them, and re-layouts: 13.2 us -> none  [local(): filtered.append(result_level.astype(jnp.bfloat16)[None])]
  transfers between devices with their start and end apart: 8 -> 17, of which waited for: 3 -> 9; matrix products, arithmetic and copies ran while one was open for 51% -> 2% of each run, Pallas kernels for 0% -> 45%
where the time goes in v1:
time: 115 us
  Pallas kernels  64.1 us (56%)
  starting transfers between devices  23.3 us (20%)
  waiting for transfers between devices  20.3 us (18%)
  local copies, waits for them, and re-layouts  3.35 us (3%)
  other arithmetic  2.77 us (2%)
    pallas_call x1, Pallas kernels, find_basis(): pl.pallas_call(basis_body, out_shape=(jax.ShapeDtypeStruct((tap_rows, ran...  30.2 us
    pallas_call x1, Pallas kernels, filter_levels(): pl.pallas_call(functools.partial(filter_body, blocks), grid=(steps,), out...  13.6 us
    ppermute x9, waiting for transfers between devices, flip_grp(): return lax.ppermute(x, 'grp', [(i, i ^ bit) for i in range(grp)])  11.8 us
    ppermute x7, starting transfers between devices, flip_bin(): return lax.ppermute(x, 'bin', [(i, i ^ bit) for i in range(bins)])  11.4 us
    ppermute x9, starting transfers between devices, flip_grp(): return lax.ppermute(x, 'grp', [(i, i ^ bit) for i in range(grp)])  9.28 us
    ppermute x7, waiting for transfers between devices, flip_bin(): return lax.ppermute(x, 'bin', [(i, i ^ bit) for i in range(bins)])  8.47 us
    pallas_call x1, Pallas kernels, make_tiles(): pl.pallas_call(functools.partial(tiles_body, levels, blocks, detectors, c...  8.22 us
    pallas_call x1, Pallas kernels, front(): pl.pallas_call(functools.partial(front_body, bins, grp), out_shape=(jax.S...  7.95 us
  transfers between devices with their start and end apart: 17, of which 9 were waited for; matrix products, arithmetic and copies ran while one was open for 2% of the time, Pallas kernels for 45%

profile of v1, /device:TPU:0, one launch (start us, length us, event | category | flops | bytes accessed | tf_op | source)
XLA Modules:
  0.0 114.7 jit_solution(6319634958771146043)
XLA Ops:
  0.7 0.6 pad_add_fusion.place_ref
  1.3 8.0 %whiten_product.1 = (bf16[1024,512]{1,0:T(8,128)(2,1)}, f32[4,256,256]{2,1,0:T(8,128)}, f32[4,256,256]{2,1,0:T(8,128)}) custom-call(s32[3]{0:T(128)} %pad_add_fusion.place_ref, s32[1,1024]{1,0:T(1,128)} %bitcast.56, s32[1,1024]{1,0:T(1,128)} %bitcast.58, f32[5,512]{1,0:T(8,128)} %gains_ref.1, bf16[1024,512]{1,0:T(8,128)(2,1)} %templates_ref.1, ...), custom_call_target="tpu_custom_call" | custom-call | tf_op jit(solution)/shard_map/whiten_product/pallas_call | solution.py:87
  9.2 0.5 collective-permute-start
  9.7 2.5 %collective-permute-done = f32[4,256,256]{2,1,0:T(8,128)S(1)} collective-permute-done((f32[4,256,256]{2,1,0:T(8,128)}, f32[4,256,256]{2,1,0:T(8,128)S(1)}, u32[]{:S(2)}, u32[]{:S(2)}) %collective-permute-start) | collective-permute-done | bytes 1048608 | tf_op jit(solution)/shard_map/ppermute | solution.py:107
  12.2 1.4 %add.67 = f32[4,256,256]{2,1,0:T(8,128)S(1)} add(f32[4,256,256]{2,1,0:T(8,128)} %get-tuple-element.18, f32[4,256,256]{2,1,0:T(8,128)S(1)} %collective-permute-done) | non-fusion elementwise | flops 262144 | bytes 3145728 | tf_op jit(solution)/shard_map/add | solution.py:111
  13.5 0.1 fusion.2
  13.6 2.9 %collective-permute-start.1 = (f32[2,128,256]{2,1,0:T(8,128)S(1)}, f32[2,128,256]{2,1,0:T(8,128)S(1)}, u32[]{:S(2)}, u32[]{:S(2)}) collective-permute-start(f32[2,128,256]{2,1,0:T(8,128)S(1)} %dynamic-slice_bitcast_fusion.1), channel_id=1, source_target_pairs={{0,8},{8,0},{16,24},{24,16},{1,9},{9,1},{17,25},{25,17},{2,10},{10... | collective-permute-start | bytes 786440 | tf_op jit(solution)/shard_map/ppermute | solution.py:103
  16.6 1.6 %collective-permute-start.3 = (f32[2,128,256]{2,1,0:T(8,128)S(1)}, f32[2,128,256]{2,1,0:T(8,128)S(1)}, u32[]{:S(2)}, u32[]{:S(2)}) collective-permute-start(f32[2,128,256]{2,1,0:T(8,128)S(1)} %dynamic-slice_bitcast_fusion), channel_id=1, source_target_pairs={{0,16},{8,24},{16,0},{24,8},{1,17},{9,25},{17,1},{25,9},{2,18},{10... | collective-permute-start | bytes 786440 | tf_op jit(solution)/shard_map/ppermute | solution.py:103
  18.2 5.0 %collective-permute-done.1 = f32[2,128,256]{2,1,0:T(8,128)S(1)} collective-permute-done((f32[2,128,256]{2,1,0:T(8,128)S(1)}, f32[2,128,256]{2,1,0:T(8,128)S(1)}, u32[]{:S(2)}, u32[]{:S(2)}) %collective-permute-start.1) | collective-permute-done | bytes 262176 | tf_op jit(solution)/shard_map/ppermute | solution.py:103
  23.2 1.8 %collective-permute-start.2 = (f32[128,256]{1,0:T(8,128)S(1)}, f32[128,256]{1,0:T(8,128)S(1)}, u32[]{:S(2)}, u32[]{:S(2)}) collective-permute-start(f32[128,256]{1,0:T(8,128)S(1)} %dynamic-slice_bitcast_fusion.3), channel_id=1, source_target_pairs={{0,16},{8,24},{16,0},{24,8},{1,17},{9,25},{17,1},{25,9},{2,18},{10... | collective-permute-start | bytes 393224 | tf_op jit(solution)/shard_map/ppermute | solution.py:103
  25.1 0.0 collective-permute-done.3
  25.1 1.6 %collective-permute-start.4 = (f32[128,256]{1,0:T(8,128)S(1)}, f32[128,256]{1,0:T(8,128)S(1)}, u32[]{:S(2)}, u32[]{:S(2)}) collective-permute-start(f32[128,256]{1,0:T(8,128)S(1)} %dynamic-slice_bitcast_fusion.2), channel_id=1, source_target_pairs={{0,8},{8,0},{16,24},{24,16},{1,9},{9,1},{17,25},{25,17},{2,10},{10... | collective-permute-start | bytes 393224 | tf_op jit(solution)/shard_map/ppermute | solution.py:103
  26.7 1.6 %collective-permute-done.2 = f32[128,256]{1,0:T(8,128)S(1)} collective-permute-done((f32[128,256]{1,0:T(8,128)S(1)}, f32[128,256]{1,0:T(8,128)S(1)}, u32[]{:S(2)}, u32[]{:S(2)}) %collective-permute-start.2) | collective-permute-done | bytes 131104 | tf_op jit(solution)/shard_map/ppermute | solution.py:103
  28.4 1.8 %collective-permute-done.4 = f32[128,256]{1,0:T(8,128)S(1)} collective-permute-done((f32[128,256]{1,0:T(8,128)S(1)}, f32[128,256]{1,0:T(8,128)S(1)}, u32[]{:S(2)}, u32[]{:S(2)}) %collective-permute-start.4) | collective-permute-done | bytes 131104 | tf_op jit(solution)/shard_map/ppermute | solution.py:103
  30.3 1.6 %collective-permute-start.5 = (f32[64,256]{1,0:T(8,128)S(1)}, f32[64,256]{1,0:T(8,128)S(1)}, u32[]{:S(2)}, u32[]{:S(2)}) collective-permute-start(f32[64,256]{1,0:T(8,128)S(1)} %get-tuple-element.29), channel_id=1, source_target_pairs={{0,2},{1,3},{2,0},{3,1},{4,6},{5,7},{6,4},{7,5},{8,10},{9,11},{10,... | collective-permute-start | bytes 196616 | tf_op jit(solution)/shard_map/ppermute | solution.py:107
  31.9 2.5 %collective-permute-start.7 = (f32[64,256]{1,0:T(8,128)S(1)}, f32[64,256]{1,0:T(8,128)S(1)}, u32[]{:S(2)}, u32[]{:S(2)}) collective-permute-start(f32[64,256]{1,0:T(8,128)S(1)} %get-tuple-element.30), channel_id=1, source_target_pairs={{0,6},{1,7},{2,4},{3,5},{4,2},{5,3},{6,0},{7,1},{8,14},{9,15},{10,... | collective-permute-start | bytes 196616 | tf_op jit(solution)/shard_map/ppermute | solution.py:107
  34.4 0.1 collective-permute-start.6
  34.5 0.8 collective-permute-done.5
  35.3 2.8 %collective-permute-done.7 = f32[64,256]{1,0:T(8,128)S(1)} collective-permute-done((f32[64,256]{1,0:T(8,128)S(1)}, f32[64,256]{1,0:T(8,128)S(1)}, u32[]{:S(2)}, u32[]{:S(2)}) %collective-permute-start.7) | collective-permute-done | bytes 65568 | tf_op jit(solution)/shard_map/ppermute | solution.py:107
  38.1 2.7 %collective-permute-done.6 = f32[64,256]{1,0:T(8,128)S(1)} collective-permute-done((f32[64,256]{1,0:T(8,128)S(1)}, f32[64,256]{1,0:T(8,128)S(1)}, u32[]{:S(2)}, u32[]{:S(2)}) %collective-permute-start.6) | collective-permute-done | bytes 65568 | tf_op jit(solution)/shard_map/ppermute | solution.py:107
  40.7 1.8 %collective-permute-start.10 = (f32[64,256]{1,0:T(8,128)S(1)}, f32[64,256]{1,0:T(8,128)S(1)}, u32[]{:S(2)}, u32[]{:S(2)}) collective-permute-start(f32[64,256]{1,0:T(8,128)S(1)} %fusion.1), channel_id=1, source_target_pairs={{0,6},{1,7},{2,4},{3,5},{4,2},{5,3},{6,0},{7,1},{8,14},{9,15},{10,... | collective-permute-start | bytes 196616 | tf_op jit(solution)/shard_map/ppermute | solution.py:107
  42.5 0.0 collective-permute-start.9
  42.5 2.7 %collective-permute-start.8 = (f32[64,256]{1,0:T(8,128)S(1)}, f32[64,256]{1,0:T(8,128)S(1)}, u32[]{:S(2)}, u32[]{:S(2)}) collective-permute-start(f32[64,256]{1,0:T(8,128)S(1)} %fusion.1), channel_id=1, source_target_pairs={{0,2},{1,3},{2,0},{3,1},{4,6},{5,7},{6,4},{7,5},{8,10},{9,11},{10,... | collective-permute-start | bytes 196616 | tf_op jit(solution)/shard_map/ppermute | solution.py:107
  45.2 1.7 %collective-permute-done.10 = f32[64,256]{1,0:T(8,128)S(1)} collective-permute-done((f32[64,256]{1,0:T(8,128)S(1)}, f32[64,256]{1,0:T(8,128)S(1)}, u32[]{:S(2)}, u32[]{:S(2)}) %collective-permute-start.10) | collective-permute-done | bytes 65568 | tf_op jit(solution)/shard_map/ppermute | solution.py:107
  46.9 1.4 %collective-permute-done.9 = f32[64,256]{1,0:T(8,128)S(1)} collective-permute-done((f32[64,256]{1,0:T(8,128)S(1)}, f32[64,256]{1,0:T(8,128)S(1)}, u32[]{:S(2)}, u32[]{:S(2)}) %collective-permute-start.9) | collective-permute-done | bytes 65568 | tf_op jit(solution)/shard_map/ppermute | solution.py:107
  48.3 0.0 collective-permute-done.8
  48.3 0.0 copy-start.2
  48.3 0.1 collective-permute-start.11
  48.4 2.6 %collective-permute-start.16 = (f32[2,2048]{1,0:T(2,128)S(1)}, f32[2,2048]{1,0:T(2,128)S(1)}, u32[]{:S(2)}, u32[]{:S(2)}) collective-permute-start(f32[2,2048]{1,0:T(2,128)S(1)} %slice.15), channel_id=1, source_target_pairs={{0,1},{1,2},{2,3},{3,4},{4,5},{5,6},{6,7},{8,9},{9,10},{10,11},{11... | collective-permute-start | bytes 49160 | tf_op jit(solution)/shard_map/ppermute | solution.py:402
  51.0 0.0 collective-permute-done.11.other_ref
  51.0 0.0 copy-start.4
  51.0 0.7 copy-done.4
  51.7 30.2 %cholesky_basis.1 = (bf16[1152,256]{1,0:T(8,128)(2,1)}, f32[1,256]{1,0:T(1,128)}) custom-call(s32[3]{0:T(128)} %pad_add_fusion.place_ref, f32[4,64,256]{2,1,0:T(8,128)} %copy-done.2, f32[4,64,256]{2,1,0:T(8,128)} %copy-done.4), custom_call_target="tpu_custom_call" | custom-call | tf_op jit(solution)/shard_map/cholesky_basis/pallas_call | solution.py:202
  81.9 1.0 slice.14.own_ref
  82.9 1.5 %collective-permute-start.14 = (bf16[256,256]{1,0:T(8,128)(2,1)S(1)}, bf16[256,256]{1,0:T(8,128)(2,1)S(1)}, u32[]{:S(2)}, u32[]{:S(2)}) collective-permute-start(bf16[256,256]{1,0:T(8,128)(2,1)S(1)} %constant_dynamic-slice_fusion), channel_id=1, source_target_pairs={{0,24},{8,16},{16,8},{24,0},{1,25},{9,17},{17,9},{25,1},{2,26},{10... | collective-permute-start | bytes 393224 | tf_op jit(solution)/shard_map/ppermute | solution.py:103
  84.4 1.5 %collective-permute-start.13 = (bf16[256,256]{1,0:T(8,128)(2,1)S(1)}, bf16[256,256]{1,0:T(8,128)(2,1)S(1)}, u32[]{:S(2)}, u32[]{:S(2)}) collective-permute-start(bf16[256,256]{1,0:T(8,128)(2,1)S(1)} %constant_dynamic-slice_fusion), channel_id=1, source_target_pairs={{0,16},{8,24},{16,0},{24,8},{1,17},{9,25},{17,1},{25,9},{2,18},{10... | collective-permute-start | bytes 393224 | tf_op jit(solution)/shard_map/ppermute | solution.py:103
  85.9 0.5 collective-permute-start.12
  86.4 0.0 collective-permute-done.16
  86.5 0.7 reshape.41.strain_ref
  87.2 8.2 %toeplitz_tiles.1.tiles_ref = bf16[8,35,128,128]{3,2,1,0:T(8,128)(2,1)} custom-call(f32[160,128]{1,0:T(8,128)} %reshape.41.strain_ref), custom_call_target="tpu_custom_call" | custom-call | flops 293601280 | bytes 9175040 | tf_op jit(solution)/shard_map/toeplitz_tiles/pallas_call | solution.py:289
  95.4 0.0 collective-permute-done.14
  95.5 0.0 copy-start.6
  95.5 0.1 collective-permute-start.15
  95.6 13.6 %filter_levels.1 = (bf16[1,2,8192,256]{3,2,1,0:T(8,128)(2,1)}, bf16[1,2,4096,256]{3,2,1,0:T(8,128)(2,1)}, bf16[1,2,2048,256]{3,2,1,0:T(8,128)(2,1)}, bf16[1,2,10...) custom-call(bf16[8,35,128,128]{3,2,1,0:T(8,128)(2,1)} %toeplitz_tiles.1.tiles_ref, bf16[1152,256]{1,0:T(8,128)(2,1)} %get-tuple-element.20.taps_ref), custom_call_target="tpu_custom_call" | custom-call | flops 8321499136 | bytes 25427968 | tf_op jit(solution)/shard_map/filter_levels/pallas_call | solution.py:329
  109.2 0.6 broadcast_multiply_fusion
  109.8 0.0 collective-permute-done.15.other_ref
  109.8 0.8 copy-done.3
  110.5 4.2 %mixing.1 = bf16[1024,256]{1,0:T(8,128)(2,1)} custom-call(s32[3]{0:T(128)} %pad_add_fusion.place_ref, s32[1,1024]{1,0:T(1,128)} %bitcast.57, bf16[1024,512]{1,0:T(8,128)(2,1)} %get-tuple-element.17.white_ref, bf16[512,256]{1,0:T(8,128)(2,1)} %copy-done, bf16[3,256,256]{2,1,0:T(8,128)(2,1)} %copy-done.1, bf16[3,256,256]{2,1,0:T(8,128)(2,1)} %copy-done.3), custom_call_target="tpu_custom_call" | custom-call | tf_op jit(solution)/shard_map/mixing/pallas_call | solution.py:376
  (27 shorter events, 0.4 us)
Async XLA Ops:
  0.6 47.8 %copy-start.5 = (f32[2,8192]{1,0:T(2,128)S(1)}, f32[2,8192]{1,0:T(2,128)}, u32[]{:S(2)}) copy-start(f32[2,8192]{1,0:T(2,128)} %param.11) | copy-start | bytes 196612
  9.2 3.0 %collective-permute-start = (f32[4,256,256]{2,1,0:T(8,128)}, f32[4,256,256]{2,1,0:T(8,128)S(1)}, u32[]{:S(2)}, u32[]{:S(2)}) collective-permute-start(f32[4,256,256]{2,1,0:T(8,128)} %get-tuple-element.19), channel_id=1, source_target_pairs={{0,1},{1,0},{2,3},{3,2},{4,5},{5,4},{6,7},{7,6},{8,9},{9,8},{10,11... | collective-permute-start | bytes 3145736 | tf_op jit(solution)/shard_map/ppermute | solution.py:107
  13.6 9.5 %collective-permute-start.1 = (f32[2,128,256]{2,1,0:T(8,128)S(1)}, f32[2,128,256]{2,1,0:T(8,128)S(1)}, u32[]{:S(2)}, u32[]{:S(2)}) collective-permute-start(f32[2,128,256]{2,1,0:T(8,128)S(1)} %dynamic-slice_bitcast_fusion.1), channel_id=1, source_target_pairs={{0,8},{8,0},{16,24},{24,16},{1,9},{9,1},{17,25},{25,17},{2,10},{10... | collective-permute-start | bytes 786440 | tf_op jit(solution)/shard_map/ppermute | solution.py:103
  16.6 8.5 %collective-permute-start.3 = (f32[2,128,256]{2,1,0:T(8,128)S(1)}, f32[2,128,256]{2,1,0:T(8,128)S(1)}, u32[]{:S(2)}, u32[]{:S(2)}) collective-permute-start(f32[2,128,256]{2,1,0:T(8,128)S(1)} %dynamic-slice_bitcast_fusion), channel_id=1, source_target_pairs={{0,16},{8,24},{16,0},{24,8},{1,17},{9,25},{17,1},{25,9},{2,18},{10... | collective-permute-start | bytes 786440 | tf_op jit(solution)/shard_map/ppermute | solution.py:103
  23.2 5.1 %collective-permute-start.2 = (f32[128,256]{1,0:T(8,128)S(1)}, f32[128,256]{1,0:T(8,128)S(1)}, u32[]{:S(2)}, u32[]{:S(2)}) collective-permute-start(f32[128,256]{1,0:T(8,128)S(1)} %dynamic-slice_bitcast_fusion.3), channel_id=1, source_target_pairs={{0,16},{8,24},{16,0},{24,8},{1,17},{9,25},{17,1},{25,9},{2,18},{10... | collective-permute-start | bytes 393224 | tf_op jit(solution)/shard_map/ppermute | solution.py:103
  25.1 5.0 %collective-permute-start.4 = (f32[128,256]{1,0:T(8,128)S(1)}, f32[128,256]{1,0:T(8,128)S(1)}, u32[]{:S(2)}, u32[]{:S(2)}) collective-permute-start(f32[128,256]{1,0:T(8,128)S(1)} %dynamic-slice_bitcast_fusion.2), channel_id=1, source_target_pairs={{0,8},{8,0},{16,24},{24,16},{1,9},{9,1},{17,25},{25,17},{2,10},{10... | collective-permute-start | bytes 393224 | tf_op jit(solution)/shard_map/ppermute | solution.py:103
  30.3 5.0 %collective-permute-start.5 = (f32[64,256]{1,0:T(8,128)S(1)}, f32[64,256]{1,0:T(8,128)S(1)}, u32[]{:S(2)}, u32[]{:S(2)}) collective-permute-start(f32[64,256]{1,0:T(8,128)S(1)} %get-tuple-element.29), channel_id=1, source_target_pairs={{0,2},{1,3},{2,0},{3,1},{4,6},{5,7},{6,4},{7,5},{8,10},{9,11},{10,... | collective-permute-start | bytes 196616 | tf_op jit(solution)/shard_map/ppermute | solution.py:107
  31.9 6.2 %collective-permute-start.7 = (f32[64,256]{1,0:T(8,128)S(1)}, f32[64,256]{1,0:T(8,128)S(1)}, u32[]{:S(2)}, u32[]{:S(2)}) collective-permute-start(f32[64,256]{1,0:T(8,128)S(1)} %get-tuple-element.30), channel_id=1, source_target_pairs={{0,6},{1,7},{2,4},{3,5},{4,2},{5,3},{6,0},{7,1},{8,14},{9,15},{10,... | collective-permute-start | bytes 196616 | tf_op jit(solution)/shard_map/ppermute | solution.py:107
  34.4 6.3 %collective-permute-start.6 = (f32[64,256]{1,0:T(8,128)S(1)}, f32[64,256]{1,0:T(8,128)S(1)}, u32[]{:S(2)}, u32[]{:S(2)}) collective-permute-start(f32[64,256]{1,0:T(8,128)S(1)} %get-tuple-element.31), channel_id=1, source_target_pairs={{0,4},{1,5},{2,6},{3,7},{4,0},{5,1},{6,2},{7,3},{8,12},{9,13},{10,... | collective-permute-start | bytes 196616 | tf_op jit(solution)/shard_map/ppermute | solution.py:107
  40.7 6.1 %collective-permute-start.10 = (f32[64,256]{1,0:T(8,128)S(1)}, f32[64,256]{1,0:T(8,128)S(1)}, u32[]{:S(2)}, u32[]{:S(2)}) collective-permute-start(f32[64,256]{1,0:T(8,128)S(1)} %fusion.1), channel_id=1, source_target_pairs={{0,6},{1,7},{2,4},{3,5},{4,2},{5,3},{6,0},{7,1},{8,14},{9,15},{10,... | collective-permute-start | bytes 196616 | tf_op jit(solution)/shard_map/ppermute | solution.py:107
  42.5 5.8 %collective-permute-start.9 = (f32[64,256]{1,0:T(8,128)S(1)}, f32[64,256]{1,0:T(8,128)S(1)}, u32[]{:S(2)}, u32[]{:S(2)}) collective-permute-start(f32[64,256]{1,0:T(8,128)S(1)} %fusion.1), channel_id=1, source_target_pairs={{0,4},{1,5},{2,6},{3,7},{4,0},{5,1},{6,2},{7,3},{8,12},{9,13},{10,... | collective-permute-start | bytes 196616 | tf_op jit(solution)/shard_map/ppermute | solution.py:107
  42.5 5.8 %collective-permute-start.8 = (f32[64,256]{1,0:T(8,128)S(1)}, f32[64,256]{1,0:T(8,128)S(1)}, u32[]{:S(2)}, u32[]{:S(2)}) collective-permute-start(f32[64,256]{1,0:T(8,128)S(1)} %fusion.1), channel_id=1, source_target_pairs={{0,2},{1,3},{2,0},{3,1},{4,6},{5,7},{6,4},{7,5},{8,10},{9,11},{10,... | collective-permute-start | bytes 196616 | tf_op jit(solution)/shard_map/ppermute | solution.py:107
  48.3 2.7 %copy-start.2 = (f32[4,64,256]{2,1,0:T(8,128)}, f32[4,64,256]{2,1,0:T(8,128)S(1)}, u32[]{:S(2)}) copy-start(f32[4,64,256]{2,1,0:T(8,128)S(1)} %pad_maximum_fusion.2.mine_ref) | copy-start | bytes 786436
  48.3 2.7 %collective-permute-start.11 = (f32[4,64,256]{2,1,0:T(8,128)S(1)}, f32[4,64,256]{2,1,0:T(8,128)S(1)}, u32[]{:S(2)}, u32[]{:S(2)}) collective-permute-start(f32[4,64,256]{2,1,0:T(8,128)S(1)} %pad_maximum_fusion.2.mine_ref), channel_id=1, source_target_pairs={{0,1},{1,0},{2,3},{3,2},{4,5},{5,4},{6,7},{7,6},{8,9},{9,8},{10,11... | collective-permute-start | bytes 786440 | tf_op jit(solution)/shard_map/ppermute | solution.py:107
  48.4 38.0 %collective-permute-start.16 = (f32[2,2048]{1,0:T(2,128)S(1)}, f32[2,2048]{1,0:T(2,128)S(1)}, u32[]{:S(2)}, u32[]{:S(2)}) collective-permute-start(f32[2,2048]{1,0:T(2,128)S(1)} %slice.15), channel_id=1, source_target_pairs={{0,1},{1,2},{2,3},{3,4},{4,5},{5,6},{6,7},{8,9},{9,10},{10,11},{11... | collective-permute-start | bytes 49160 | tf_op jit(solution)/shard_map/ppermute | solution.py:402
  51.0 0.7 copy-start.4
  82.8 26.3 %copy-start = (bf16[512,256]{1,0:T(8,128)(2,1)}, bf16[512,256]{1,0:T(8,128)(2,1)S(1)}, u32[]{:S(2)}) copy-start(bf16[512,256]{1,0:T(8,128)(2,1)S(1)} %slice.14.own_ref) | copy-start | bytes 786436
  82.9 12.5 %collective-permute-start.14 = (bf16[256,256]{1,0:T(8,128)(2,1)S(1)}, bf16[256,256]{1,0:T(8,128)(2,1)S(1)}, u32[]{:S(2)}, u32[]{:S(2)}) collective-permute-start(bf16[256,256]{1,0:T(8,128)(2,1)S(1)} %constant_dynamic-slice_fusion), channel_id=1, source_target_pairs={{0,24},{8,16},{16,8},{24,0},{1,25},{9,17},{17,9},{25,1},{2,26},{10... | collective-permute-start | bytes 393224 | tf_op jit(solution)/shard_map/ppermute | solution.py:103
  84.4 11.0 %collective-permute-start.13 = (bf16[256,256]{1,0:T(8,128)(2,1)S(1)}, bf16[256,256]{1,0:T(8,128)(2,1)S(1)}, u32[]{:S(2)}, u32[]{:S(2)}) collective-permute-start(bf16[256,256]{1,0:T(8,128)(2,1)S(1)} %constant_dynamic-slice_fusion), channel_id=1, source_target_pairs={{0,16},{8,24},{16,0},{24,8},{1,17},{9,25},{17,1},{25,9},{2,18},{10... | collective-permute-start | bytes 393224 | tf_op jit(solution)/shard_map/ppermute | solution.py:103
  85.9 9.5 %collective-permute-start.12 = (bf16[256,256]{1,0:T(8,128)(2,1)S(1)}, bf16[256,256]{1,0:T(8,128)(2,1)S(1)}, u32[]{:S(2)}, u32[]{:S(2)}) collective-permute-start(bf16[256,256]{1,0:T(8,128)(2,1)S(1)} %constant_dynamic-slice_fusion), channel_id=1, source_target_pairs={{0,8},{8,0},{16,24},{24,16},{1,9},{9,1},{17,25},{25,17},{2,10},{10... | collective-permute-start | bytes 393224 | tf_op jit(solution)/shard_map/ppermute | solution.py:103
  95.5 13.7 %copy-start.1 = (bf16[3,256,256]{2,1,0:T(8,128)(2,1)}, bf16[3,256,256]{2,1,0:T(8,128)(2,1)S(1)}, u32[]{:S(2)}) copy-start(bf16[3,256,256]{2,1,0:T(8,128)(2,1)S(1)} %pad_maximum_fusion.mine_ref) | copy-start | bytes 1179652
  95.5 13.7 %copy-start.6 = (f32[1,256]{1,0:T(1,128)S(1)}, f32[1,256]{1,0:T(1,128)}, u32[]{:S(2)}) copy-start(f32[1,256]{1,0:T(1,128)} %get-tuple-element.21) | copy-start | bytes 3076
  95.5 14.3 %collective-permute-start.15 = (bf16[3,256,256]{2,1,0:T(8,128)(2,1)S(1)}, bf16[3,256,256]{2,1,0:T(8,128)(2,1)S(1)}, u32[]{:S(2)}, u32[]{:S(2)}) collective-permute-start(bf16[3,256,256]{2,1,0:T(8,128)(2,1)S(1)} %pad_maximum_fusion.mine_ref), channel_id=1, source_target_pairs={{0,1},{1,0},{2,3},{3,2},{4,5},{5,4},{6,7},{7,6},{8,9},{9,8},{10,11... | collective-permute-start | bytes 1179656 | tf_op jit(solution)/shard_map/ppermute | solution.py:107
  109.8 0.8 copy-start.3

commit v2 on v0

v2 whole, which is shorter than its diff:
```python
import functools
import math

import jax
import jax.numpy as jnp
from jax import lax
from jax.experimental import pallas as pl
from jax.experimental.pallas import tpu as pltpu
from jax.sharding import PartitionSpec as P

highest = lax.Precision.HIGHEST
inv_root_two = 0.7071067811865476
f32 = jnp.float32
bf16 = jnp.bfloat16
LANES = 128
SUBLANES = 8
MIB = 1024 * 1024


def iota(shape, axis):
    return lax.broadcasted_iota(jnp.int32, shape, axis)


def split3(x):
    high = x.astype(bf16)
    rest = x - high.astype(f32)
    middle = rest.astype(bf16)
    low = (rest - middle.astype(f32)).astype(bf16)
    return high, middle, low


def split2(x):
    high = x.astype(bf16)
    return high, (x - high.astype(f32)).astype(bf16)


def dot(a, b, precision=None):
    return jnp.dot(a, b, preferred_element_type=f32, precision=precision)


def dot_t(a, b, precision=None):
    return lax.dot_general(
        a, b, (((0,), (0,)), ((), ())), preferred_element_type=f32, precision=precision
    )


def params(mib):
    return pltpu.CompilerParams(vmem_limit_bytes=mib * MIB)


def spread(group, rows, groups, width):
    member = (iota((8, rows), 0) == group).astype(f32).astype(bf16)
    column = (iota((8, groups * width), 0) == iota((8, groups * width), 1) // width).astype(f32)
    return dot_t(member, column.astype(bf16))


def front_body(bins, grp, owner_ref, code_ref, gains_hbm, templates_hbm, sketch_hbm, white_hbm, keep_hbm,
               send_hbm, gains_ref, templates_ref, sketch_ref, white_ref, sketched_ref, keep_ref, send_ref,
               sem, out_sem):
    rows, width = templates_ref.shape
    rates = gains_ref.shape[0]
    pieces = 4
    piece = rows // pieces
    copies = [
        pltpu.make_async_copy(gains_hbm, gains_ref, sem.at[0]),
        pltpu.make_async_copy(sketch_hbm, sketch_ref, sem.at[1]),
    ]
    for i in range(pieces):
        at = pl.ds(i * piece, piece)
        copies.append(
            pltpu.make_async_copy(templates_hbm.at[at], templates_ref.at[at], sem.at[2 + i])
        )
    for copy in copies:
        copy.start()
    given = [
        pltpu.make_async_copy(white_ref, white_hbm, out_sem.at[0]),
        pltpu.make_async_copy(send_ref, send_hbm, out_sem.at[1]),
        pltpu.make_async_copy(keep_ref, keep_hbm, out_sem.at[2]),
    ]
    member = (iota((8, rows), 0) == code_ref[...]).astype(f32)
    member = jnp.concatenate([member, member, member], axis=0).astype(bf16)
    mask = spread(owner_ref[...] // grp, rows, bins, LANES).astype(bf16)
    copies[0].wait()
    gains = jnp.concatenate([gains_ref[...], jnp.zeros((8 - rates, width), f32)], axis=0)
    parts = jnp.concatenate([part.astype(f32) for part in split3(gains)], axis=0).astype(bf16)
    copies[1].wait()
    sketch_parts = split2(sketch_ref[...])
    for i in range(pieces):
        at = slice(i * piece, (i + 1) * piece)
        factor = dot_t(member[:, at], parts)
        copies[2 + i].wait()
        white = (templates_ref[at, :].astype(f32) * factor).astype(bf16)
        white_ref[at, :] = white
        sketched = None
        for part in sketch_parts:
            term = dot(white, part)
            sketched = term if sketched is None else sketched + term
        sketched_ref[at, :] = sketched
    given[0].start()
    core = lax.axis_index("grp") % 2
    sketched_parts = split2(sketched_ref[...])
    products(bins, 1 - core, mask, white_ref, sketched_parts, send_ref)
    given[1].start()
    products(bins, core, mask, white_ref, sketched_parts, keep_ref)
    given[2].start()
    for copy in given:
        copy.wait()


def products(bins, which, mask, white_ref, sketched_parts, out_ref):
    rows, width = white_ref.shape
    half = width // 2
    chosen = white_ref[:, pl.ds(pl.multiple_of(which * half, half), half)]
    masked = jnp.concatenate(
        [
            chosen * jnp.concatenate([mask[:, b * LANES : (b + 1) * LANES]] * (half // LANES), axis=1)
            for b in range(bins)
        ],
        axis=1,
    )
    total = None
    for part in sketched_parts:
        term = dot_t(masked, part)
        total = term if total is None else total + term
    for b in range(bins):
        high, low = b // 2, b % 2
        one, two = jnp.where(which == 0, low, high), jnp.where(which == 0, high, low)
        for i in range(out_ref.shape[0]):
            out_ref[i, one, two] = total[b * half : (b + 1) * half, i * LANES : (i + 1) * LANES]


def halves(bins, width, rank):
    return (rank // LANES, 2, bins // 2, width // 2, LANES)


def front(owner, code, gains, templates, sketch, bins, grp):
    rows, width = templates.shape
    rank = sketch.shape[1]
    vmem, anywhere = pl.BlockSpec(memory_space=pltpu.VMEM), pl.BlockSpec(memory_space=pl.ANY)
    sent = halves(bins, width, rank)
    return pl.pallas_call(
        functools.partial(front_body, bins, grp),
        out_shape=(
            jax.ShapeDtypeStruct((rows, width), bf16),
            jax.ShapeDtypeStruct(sent, f32),
            jax.ShapeDtypeStruct(sent, f32),
        ),
        in_specs=[vmem, vmem, anywhere, anywhere, anywhere],
        out_specs=(anywhere, anywhere, anywhere),
        scratch_shapes=[
            pltpu.VMEM(gains.shape, f32),
            pltpu.VMEM(templates.shape, bf16),
            pltpu.VMEM(sketch.shape, f32),
            pltpu.VMEM((rows, width), bf16),
            pltpu.VMEM((rows, rank), f32),
            pltpu.VMEM(sent, f32),
            pltpu.VMEM(sent, f32),
            pltpu.SemaphoreType.DMA((6,)),
            pltpu.SemaphoreType.DMA((3,)),
        ],
        compiler_params=params(60),
        name="whiten_products",
    )(owner, code, gains, templates, sketch)


def pick(x, index):
    return lax.dynamic_index_in_dim(x, index, 0, keepdims=False)


def flip_bin(x, bits, bins, grp):
    pairs = [
        (b * grp + g, (b ^ bits[g % 2]) * grp + g) for b in range(bins) for g in range(grp)
    ]
    return lax.ppermute(x, ("bin", "grp"), pairs)


def flip_core(x, grp):
    return lax.ppermute(x, "grp", [(i, i ^ 1) for i in range(grp)])


def flip_chip(x, bits, grp):
    return lax.ppermute(x, "grp", [(i, i ^ (2 * bits[i % 2])) for i in range(grp)])


def reduce_products(keep, send, bins, grp, beside):
    keep, done = beside[0](keep, ())
    came = flip_core(send, grp)
    came, *done = lax.optimization_barrier((came, *done))
    came, done = beside[1](came, done)
    here = lax.axis_index("bin")
    core = lax.axis_index("grp") % 2
    high, low = here >> 1, here & 1
    one, two = jnp.where(core == 0, low, high), jnp.where(core == 0, high, low)
    pieces = range(keep.shape[0])

    def stage(held, leaving, move):
        arrived = [move(x) for x in leaving]
        return [x + y for x, y in zip(held, arrived)]

    total = stage(
        [pick(keep[i], one) + pick(came[i], one) for i in pieces],
        [pick(keep[i], 1 - one) + pick(came[i], 1 - one) for i in pieces],
        lambda x: flip_bin(x, (1, 2), bins, grp),
    )
    *total, done_0, done_1 = lax.optimization_barrier((*total, *done))
    total[-1], done = beside[2](total[-1], (done_0, done_1))
    mine = stage(
        [pick(x, two) for x in total],
        [pick(x, 1 - two) for x in total],
        lambda x: flip_bin(x, (2, 1), bins, grp),
    )
    bits = [1 << i for i in range((grp // 2).bit_length() - 1)]
    mine[-1], *done = lax.optimization_barrier((mine[-1], *done))
    for step, bit in enumerate(bits):
        mine = stage(mine, mine, lambda x: flip_chip(x, (bit, bits[-1 - step]), grp))
    return mine, [flip_core(x, grp) for x in mine], done


def eliminate(state):
    finished = []
    size = state.shape[0]
    head = iota((SUBLANES, size), 0)
    for start in range(0, size, SUBLANES):
        lane = iota(state.shape, 1)
        columns = [
            jnp.broadcast_to(state[:, start + k : start + k + 1], state.shape)
            for k in range(SUBLANES)
        ]
        state = jnp.where((lane >= start) & (lane < start + SUBLANES), f32(0.0), state)
        eye = iota((SUBLANES, size), 1) == head + start
        top = jnp.where(eye, f32(1.0), state[:SUBLANES])
        rest = state[SUBLANES:]
        more = rest.shape[0] > 0
        tops = [column[:SUBLANES] for column in columns]
        rests = [column[SUBLANES:] for column in columns]
        pivots = jnp.zeros((SUBLANES, size), f32)
        for k in range(SUBLANES):
            pivot = tops[k][k : k + 1]
            inverse = 1.0 / pivot
            below = jnp.where(head > k, tops[k], f32(0.0))
            factor = rests[k] * inverse if more else None
            for j in range(k + 1, SUBLANES):
                across = tops[j][k : k + 1]
                tops[j] = tops[j] - (below * across) * inverse
                if more:
                    rests[j] = rests[j] - factor * across
            across = top[k : k + 1]
            top = top - (below * across) * inverse
            if more:
                rest = rest - factor * across
            pivots = jnp.where(head == k, pivot, pivots)
        finished.append(top * lax.rsqrt(pivots))
        state = rest
    inverse = jnp.concatenate(finished, axis=0)
    return jnp.where(iota((size, size), 0) >= iota((size, size), 1), inverse, f32(0.0))


def joined_rows(mine_ref, other_ref, product_ref):
    half = mine_ref.shape[0]
    core = lax.axis_index("grp") % 2
    product_ref[pl.ds(pl.multiple_of(core * half, half), half), :] = mine_ref[...]
    product_ref[pl.ds(pl.multiple_of((1 - core) * half, half), half), :] = other_ref[...]
    return product_ref[...]


def basis_piece(scale_down, product, before):
    inner = dot_t(product, product, highest)
    rest = product
    for basis in before:
        across = dot_t(basis, product, highest)
        inner = inner - dot_t(across, across, highest)
        rest = rest - dot(basis, across, highest)
    inverse = eliminate(inner)
    basis = lax.dot_general(
        rest, inverse, (((1,), (1,)), ((), ())), preferred_element_type=f32, precision=highest
    )
    eye = iota(inverse.shape, 0) == iota(inverse.shape, 1)
    diagonal = jnp.sum(jnp.where(eye, inverse, f32(0.0)), axis=0, keepdims=True)
    return basis, (1.0 / diagonal) / scale_down


def piece_body(scale_down, mine_ref, other_ref, basis_ref, spectrum_ref, product_ref):
    product = joined_rows(mine_ref, other_ref, product_ref)
    basis_ref[...], spectrum_ref[...] = basis_piece(scale_down, product, [])


def first_piece(mine, other, scale_down):
    half, columns = mine.shape
    return pl.pallas_call(
        functools.partial(piece_body, scale_down),
        out_shape=(
            jax.ShapeDtypeStruct((2 * half, columns), f32),
            jax.ShapeDtypeStruct((1, columns), f32),
        ),
        scratch_shapes=[pltpu.VMEM((2 * half, columns), f32)],
        compiler_params=params(8),
        name="basis_first",
    )(mine, other)


def basis_body(scale_down, first_ref, first_spectrum_ref, mine_ref, other_ref, own_ref, part_ref, taps_ref,
               spectrum_ref, product_ref, wide_ref):
    half = mine_ref.shape[0]
    core = lax.axis_index("grp") % 2
    product = joined_rows(mine_ref, other_ref, product_ref)
    first = first_ref[...]
    wide_ref[0] = first
    wide_ref[1], spectrum_ref[:, LANES:] = basis_piece(scale_down, product, [first])
    spectrum_ref[:, :LANES] = first_spectrum_ref[...]
    own_ref[...] = jnp.concatenate([wide_ref[0], wide_ref[1]], axis=1).astype(bf16)
    part_ref[...] = own_ref[pl.ds(pl.multiple_of(core * half, half), half), :]
    at = 0
    taps, level = half, 1
    while at < taps_ref.shape[0]:
        rows = max(taps, LANES)
        chosen = jnp.concatenate(
            [wide_ref[part, pl.ds(0, taps, stride=2**level), :] for part in range(2)], axis=1
        )
        if rows > taps:
            chosen = jnp.concatenate([chosen, jnp.zeros((rows - taps, 2 * LANES), f32)], axis=0)
        taps_ref[at : at + rows, :] = chosen.astype(bf16)
        at, taps, level = at + rows, taps // 2, level + 1


def find_basis(mine, other, tap_rows, scale_down):
    first, first_spectrum = first_piece(mine[0], other[0], scale_down)
    half = mine[0].shape[0]
    length, rank = 2 * half, 2 * LANES
    return pl.pallas_call(
        functools.partial(basis_body, scale_down),
        out_shape=(
            jax.ShapeDtypeStruct((length, rank), bf16),
            jax.ShapeDtypeStruct((half, rank), bf16),
            jax.ShapeDtypeStruct((tap_rows, rank), bf16),
            jax.ShapeDtypeStruct((1, rank), f32),
        ),
        scratch_shapes=[pltpu.VMEM((length, LANES), f32), pltpu.VMEM((2, length, LANES), f32)],
        compiler_params=params(8),
        name="basis_second",
    )(first, first_spectrum, mine[1], other[1])


def level_sizes(levels, tap_count):
    return [max(1, (tap_count >> r) // LANES) for r in range(levels)]


def level_starts(total, levels):
    starts = [0]
    for r in range(levels):
        starts.append(starts[-1] + (total >> r))
    return starts


def levels_body(levels, detectors, history_ref, strain_ref, flipped_ref, level_ref):
    lead = history_ref.shape[1] // LANES
    each = lead + strain_ref.shape[1] // LANES
    total = detectors * each
    starts = level_starts(total, levels)
    source = iota((2 * LANES, 2 * LANES), 0)
    target = iota((2 * LANES, 2 * LANES), 1)
    even_odd = (source == 2 * (target % LANES) + target // LANES).astype(f32).astype(bf16)
    reverse = (
        iota((LANES, LANES), 0) + iota((LANES, LANES), 1) == LANES - 1
    ).astype(f32).astype(bf16)
    for d in range(detectors):
        for q in range(each):
            from_ref, at = (history_ref, q) if q < lead else (strain_ref, q - lead)
            level_ref[d * each + q : d * each + q + 1, :] = from_ref[
                d : d + 1, at * LANES : (at + 1) * LANES
            ]
    for r in range(levels):
        rows = total >> r
        at = starts[r]
        if r > 0:
            before = starts[r - 1]
            joined = jnp.concatenate(
                [
                    level_ref[pl.ds(before, rows, stride=2), :],
                    level_ref[pl.ds(before + 1, rows, stride=2), :],
                ],
                axis=1,
            )
            high, middle, low = split3(joined)
            both = (dot(high, even_odd) + dot(middle, even_odd)) + dot(low, even_odd)
            level_ref[at : at + rows, :] = (both[:, :LANES] + both[:, LANES:]) * inv_root_two
        rounded = level_ref[at : at + rows, :].astype(bf16)
        flipped_ref[at : at + rows, :] = dot(rounded, reverse)


def flipped_levels(history, strain, levels):
    detectors = strain.shape[0]
    total = detectors * (history.shape[1] + strain.shape[1]) // LANES
    held = -(-level_starts(total, levels)[-1] // SUBLANES) * SUBLANES
    return pl.pallas_call(
        functools.partial(levels_body, levels, detectors),
        out_shape=jax.ShapeDtypeStruct((held, LANES), f32),
        scratch_shapes=[pltpu.VMEM((held, LANES), f32)],
        compiler_params=params(6),
        name="strain_levels",
    )(history, strain)


def tiles_body(wanted, total, levels, blocks, detectors, chunks, flipped_ref, tiles_ref):
    step = pl.program_id(0)
    starts = level_starts(total, levels)
    detector = step // chunks
    chunk = step % chunks
    lower = iota((LANES, LANES), 1) <= iota((LANES, LANES), 0)
    at = 0
    for r in wanted:
        rows = (total >> r) // detectors
        history = (1 << (levels - 1)) >> r
        count = (rows - history) // chunks
        first = starts[r] + detector * rows + history + chunk * count - (blocks[r] - 1)

        def turned(row):
            line = jnp.broadcast_to(flipped_ref[pl.ds(row, 1), :], (LANES, LANES))
            return pltpu.roll(line, 1, 1, stride=1, stride_axis=0)

        before = turned(first - 1)
        for i in range(count + blocks[r] - 1):
            now = turned(first + i)
            tiles_ref[0, at] = jnp.where(lower, now, before).astype(bf16)
            before = now
            at += 1


def make_tiles(flipped, total, wanted, levels, blocks, detectors, chunks):
    count = 0
    for r in wanted:
        rows = (total >> r) // detectors
        lead = (1 << (levels - 1)) >> r
        count += (rows - lead) // chunks + blocks[r] - 1
    steps = detectors * chunks
    return pl.pallas_call(
        functools.partial(tiles_body, wanted, total, levels, blocks, detectors, chunks),
        grid=(steps,),
        out_shape=jax.ShapeDtypeStruct((steps, count, LANES, LANES), bf16),
        in_specs=[pl.BlockSpec(flipped.shape, lambda i: (0, 0))],
        out_specs=pl.BlockSpec((1, count, LANES, LANES), lambda i: (i, 0, 0, 0)),
        compiler_params=params(6),
        cost_estimate=pl.CostEstimate(
            flops=steps * count * LANES * LANES * 64,
            bytes_accessed=steps * count * LANES * LANES * 2, transcendentals=0,
        ),
        name="toeplitz_tiles",
    )(flipped)


def filter_body(blocks, chunks, unroll, tiles_ref, taps_ref, *refs):
    count = len(blocks)
    out_refs, held_refs = refs[:count], refs[count : 2 * count]
    here_ref, out_sem = tiles_ref, refs[2 * count]
    steps = tiles_ref.shape[0]

    def give(step, r):
        rows = out_refs[r].shape[2] // chunks
        spot = (step // chunks, pl.ds(step % chunks * rows, rows))
        return pltpu.make_async_copy(
            held_refs[r].at[spot], out_refs[r].at[(0, *spot)], out_sem.at[step, r]
        )

    def work(step):
        at, tap_at = 0, 0
        for r in range(count):
            rows = out_refs[r].shape[2] // chunks
            b = blocks[r]
            taps = taps_ref[tap_at : tap_at + b * LANES, :]
            group = min(rows, 512)
            for i in range(0, rows, group):
                first = at + b - 1 + i // LANES
                columns = [
                    here_ref[step, first - k : first - k + group // LANES].reshape(group, LANES)
                    for k in range(b)
                ]
                joined = jnp.concatenate(columns, axis=1) if b > 1 else columns[0]
                place = pl.ds(step % chunks * rows + i, group)
                held_refs[r][step // chunks, place, :] = dot(joined, taps).astype(bf16)
            give(step, r).start()
            at += rows // LANES + b - 1
            tap_at += b * LANES

    if unroll:
        for step in range(steps):
            work(step)
    else:
        pl.loop(0, steps)(work)
    for step in range(steps):
        for r in range(count):
            give(step, r).wait()


def filter_levels(tiles, taps, lengths, blocks, detectors, chunks, unroll=True):
    rank = taps.shape[1]
    steps = tiles.shape[0]
    anywhere = pl.BlockSpec(memory_space=pl.ANY)
    return pl.pallas_call(
        functools.partial(filter_body, blocks, chunks, unroll),
        out_shape=[jax.ShapeDtypeStruct((1, detectors, n, rank), bf16) for n in lengths],
        in_specs=[pl.BlockSpec(memory_space=pltpu.VMEM)] * 2,
        out_specs=[anywhere] * len(lengths),
        scratch_shapes=[pltpu.VMEM((detectors, n, rank), bf16) for n in lengths]
        + [pltpu.SemaphoreType.DMA((steps, len(lengths)))],
        compiler_params=params(18),
        cost_estimate=pl.CostEstimate(
            flops=2 * sum(n * b for n, b in zip(lengths, blocks)) * LANES * rank * detectors,
            bytes_accessed=2 * detectors * sum(lengths) * rank + 2 * math.prod(tiles.shape),
            transcendentals=0,
        ),
        name="filter_levels",
    )(tiles, taps)


def mixing_body(bins, grp, owner_ref, white_ref, own_ref, mine_ref, other_ref, out_ref, bases_ref):
    rows, width = white_ref.shape
    rank = own_ref.shape[1]
    half = width // 2
    core, here = lax.axis_index("grp") % 2, lax.axis_index("bin")
    bases_ref[0] = own_ref[...]
    bases_ref[1 + core] = mine_ref[:width]
    bases_ref[2 - core] = other_ref[:width]
    bases_ref[3, pl.ds(pl.multiple_of(core * half, half), half), :] = mine_ref[width:]
    bases_ref[3, pl.ds(pl.multiple_of((1 - core) * half, half), half), :] = other_ref[width:]
    mask = spread((owner_ref[...] // grp) ^ here, rows, bins, rank)
    white = white_ref[...]
    total = None
    for m in range(bins):
        chosen = mask[:, m * rank : (m + 1) * rank] > 0.5
        term = jnp.where(chosen, dot(white, bases_ref[m]), f32(0.0))
        total = term if total is None else total + term
    out_ref[...] = total.astype(bf16)


def mix(owner, white, own, mine, other, bins, grp):
    rows, width = white.shape
    rank = own.shape[1]
    return pl.pallas_call(
        functools.partial(mixing_body, bins, grp),
        out_shape=jax.ShapeDtypeStruct((rows, rank), bf16),
        scratch_shapes=[pltpu.VMEM((bins, width, rank), bf16)],
        compiler_params=params(14),
        name="mixing",
    )(owner, white, own, mine, other)


def local(templates, owner_device, rate_code, rate_gains, sketch, strain):
    rows, width = templates.shape
    grp = lax.axis_size("grp")
    bins = lax.axis_size("bin")
    levels = rate_gains.shape[0]
    detectors, samples = strain.shape
    owner = owner_device.reshape(1, rows)

    blocks = level_sizes(levels, width)
    chunks = 4
    reach = LANES << (levels - 1)
    total = detectors * (reach + samples) // LANES
    white, keep, send = front(
        owner, rate_code.reshape(1, rows), rate_gains, templates, sketch, bins, grp
    )

    def before(x, done):
        x, here = lax.optimization_barrier((x, strain))
        history = lax.ppermute(here[:, -reach:], "grp", [(i, i + 1) for i in range(grp - 1)])
        return x, (history,)

    def fine(x, done):
        x, history = lax.optimization_barrier((x, *done))
        flipped = flipped_levels(history, strain, levels)
        return x, (flipped, tiles_of(flipped, (0,)))

    def coarse(x, done):
        x, flipped, tiles = lax.optimization_barrier((x, *done))
        return x, (tiles, tiles_of(flipped, tuple(range(1, levels))))

    def tiles_of(flipped, wanted):
        return make_tiles(flipped, total, wanted, levels, blocks, detectors, chunks)

    mine, other, (tiles_fine, tiles_coarse) = reduce_products(
        keep, send, bins, grp, (before, fine, coarse)
    )
    own, part, taps, spectrum = find_basis(
        mine, other, sum(blocks[1:]) * LANES, rows * grp * math.sqrt(width)
    )
    near = flip_bin(own, (1, 2), bins, grp)
    far = flip_bin(part, (3, 3), bins, grp)
    lengths = [samples >> r for r in range(levels)]
    (finest,) = filter_levels(tiles_fine, own, lengths[:1], blocks[:1], detectors, chunks)
    near, far, finest = lax.optimization_barrier((near, far, finest))
    theirs = jnp.concatenate([near, far], axis=0)
    theirs_other = flip_core(theirs, grp)
    taps, theirs = lax.optimization_barrier((taps, theirs))
    filtered = filter_levels(tiles_coarse, taps, lengths[1:], blocks[1:], detectors, chunks)
    mixing = mix(owner, white, own, theirs, theirs_other, bins, grp)
    return (mixing, spectrum, finest, *filtered)


def solution(mesh):
    return jax.shard_map(
        local,
        mesh=mesh,
        in_specs=(
            P(("bin", "grp"), None),
            P(("bin", "grp"), None),
            P(("bin", "grp")),
            P(),
            P(),
            P(None, "grp"),
        ),
        out_specs=(
            P(("bin", "grp"), None),
            P("bin", None),
            P("bin", None, "grp", None),
            P("bin", None, "grp", None),
            P("bin", None, "grp", None),
            P("bin", None, "grp", None),
            P("bin", None, "grp", None),
        ),
        check_vma=False,
    )
```

time: 455 us -> 71.9 us (0.16); the launches traced: 447 us -> 71.2 us
  matrix products: 179 us -> 0 us
  other arithmetic: 88.3 us -> 0.24 us
  local copies, waits for them, and re-layouts: 71.7 us -> 4.41 us
  waiting for transfers between devices: 67.2 us -> 8.61 us
  Pallas kernels: 0 us -> 35 us
  between operations: 16.3 us -> 0.91 us
    conv_general_dilated x5 -> x0, matrix products: 166 us -> none  [filter_level(): lax.conv_general_dilated(joined[:, :, None], tap_rows[::-1][:, None, :],...]
    another operation x12 -> x0, other arithmetic: 63.2 us -> none  [the longest x6 34.3 us: basis_from(): lower_factor = jnp.linalg.cholesky(inner_gram)]
    psum x1 -> x0, waiting for transfers between devices: 59 us -> none  [local(): gram_total = lax.psum(partial_gram, 'grp')]
    pallas_call x0 -> x9, Pallas kernels: none -> 35 us  [the longest x2 9.48 us: filter_levels(): pl.pallas_call(functools.partial(filter_body, blocks, chunks, unroll), ou...]
    broadcast_in_dim x15 -> x0, local copies, waits for them, and re-layouts: 14 us -> none  [the longest x5 12.9 us: local(): filtered.append(result_level.astype(jnp.bfloat16)[None])]
    convert_element_type x6 -> x0, local copies, waits for them, and re-layouts: 13.2 us -> none  [local(): filtered.append(result_level.astype(jnp.bfloat16)[None])]
    slice x15 -> x3, local copies, waits for them, and re-layouts: 14.2 us -> 2.06 us  [the longest x1 1.27 us: reduce_products(): keep[i]]
    all_to_all x2 -> x0, starting transfers between devices: 11.1 us -> none  [the longest x1 7.43 us: local(): lax.all_to_all(outgoing, ('bin', 'grp'), split_axis=0, concat_axis=0, til...]
  transfers between devices with their start and end apart: 8 -> 15, of which waited for: 3 -> 6; matrix products, arithmetic and copies ran while one was open for 51% -> 3% of each run, Pallas kernels for 0% -> 27%
where the time goes in v2:
time: 71.9 us; the launch traced here: 71.2 us
  Pallas kernels  35 us (49%)
  starting transfers between devices  22 us (31%)
  waiting for transfers between devices  8.61 us (12%)
  local copies, waits for them, and re-layouts  4.41 us (6%)
  between operations  0.91 us (1%)
    ppermute x4, starting transfers between devices, flip_chip(): lax.ppermute(x, 'grp', [(i, i ^ 2 * bits[i % 2]) for i in range(grp)])  11 us
    pallas_call x2, Pallas kernels, filter_levels(): pl.pallas_call(functools.partial(filter_body, blocks, chunks, unroll), ou...  9.48 us
    ppermute x6, starting transfers between devices, flip_bin(): return lax.ppermute(x, ('bin', 'grp'), pairs)  8.29 us
    pallas_call x1, Pallas kernels, front(): pl.pallas_call(functools.partial(front_body, bins, grp), out_shape=(jax.S...  7.4 us
    pallas_call x1, Pallas kernels, find_basis(): pl.pallas_call(functools.partial(basis_body, scale_down), out_shape=(jax....  5.61 us
    ppermute x4, waiting for transfers between devices, flip_chip(): lax.ppermute(x, 'grp', [(i, i ^ 2 * bits[i % 2]) for i in range(grp)])  5.26 us
    pallas_call x1, Pallas kernels, first_piece(): pl.pallas_call(functools.partial(piece_body, scale_down), out_shape=(jax....  4.59 us
    pallas_call x2, Pallas kernels, make_tiles(): pl.pallas_call(functools.partial(tiles_body, wanted, total, levels, block...  4.25 us
  transfers between devices with their start and end apart: 15, of which 6 were waited for; matrix products, arithmetic and copies ran while one was open for 3% of the time, Pallas kernels for 27%

profile of v2, /device:TPU:0, one launch (start us, length us, event | category | flops | bytes accessed | tf_op | source)
XLA Modules:
  0.0 71.2 jit_solution(1731858117395816916)
XLA Ops:
  0.6 0.0 copy-start.3
  0.6 7.4 %whiten_products.1 = (bf16[1024,512]{1,0:T(8,128)(2,1)}, f32[2,2,2,256,128]{4,3,2,1,0:T(8,128)}, f32[2,2,2,256,128]{4,3,2,1,0:T(8,128)}) custom-call(s32[1,1024]{1,0:T(1,128)} %bitcast.18, s32[1,1024]{1,0:T(1,128)} %bitcast.20, f32[5,512]{1,0:T(8,128)} %gains_hbm.1, bf16[1024,512]{1,0:T(8,128)(2,1)} %templates_hbm.1, f32[512,256]{1,0:T(8,128)} %sketch_hbm.1), custom_call_target="tpu_custom_call" | custom-call | tf_op jit(solution)/shard_map/whiten_products/pallas_call | solution.py:141
  8.1 0.5 collective-permute-start
  8.6 0.7 %slice.20 = f32[2,2048]{1,0:T(2,128)S(1)} slice(f32[2,8192]{1,0:T(2,128)} %strain_ref.1), slice={[0:2], [6144:8192]} | slice | bytes 32768 | tf_op jit(solution)/shard_map/slice | solution.py:564
  9.3 2.0 %collective-permute-start.1 = (f32[2,2048]{1,0:T(2,128)S(1)}, f32[2,2048]{1,0:T(2,128)S(1)}, u32[]{:S(2)}, u32[]{:S(2)}) collective-permute-start(f32[2,2048]{1,0:T(2,128)S(1)} %slice.20), channel_id=1, source_target_pairs={{0,1},{1,2},{2,3},{3,4},{4,5},{5,6},{6,7},{8,9},{9,10},{10,11},{11... | collective-permute-start | bytes 49160 | tf_op jit(solution)/shard_map/ppermute | solution.py:564
  11.2 1.3 %fusion = (f32[1,2,2,256,128]{4,3,2,1,0:T(8,128)S(1)}, f32[1,2,2,256,128]{4,3,2,1,0:T(8,128)S(1)}) fusion(f32[2,2,2,256,128]{4,3,2,1,0:T(8,128)} %get-tuple-element.41), kind=kLoop, calls=%fused_computation.10 | loop fusion | bytes 2097152 | tf_op jit(solution)/shard_map/slice | solution.py:201
  12.5 0.0 collective-permute-done.1.history_ref
  12.6 0.0 collective-permute-done
  12.6 0.1 fusion.1
  12.7 3.0 %collective-permute-start.2 = (f32[2,256,128]{2,1,0:T(8,128)S(1)}, f32[2,256,128]{2,1,0:T(8,128)S(1)}, u32[]{:S(2)}, u32[]{:S(2)}) collective-permute-start(f32[2,256,128]{2,1,0:T(8,128)S(1)} %add_bitcast_fusion.1), channel_id=1, source_target_pairs={{0,8},{1,17},{2,10},{3,19},{4,12},{5,21},{6,14},{7,23},{8,0},{9,25... | collective-permute-start | bytes 786440 | tf_op jit(solution)/shard_map/ppermute | solution.py:174
  15.7 0.1 collective-permute-start.3
  15.8 0.0 copy-done.3
  15.8 1.0 %strain_levels.1.flipped_ref = f32[312,128]{1,0:T(8,128)S(1)} custom-call(f32[2,2048]{1,0:T(2,128)S(1)} %collective-permute-done.1.history_ref, f32[2,8192]{1,0:T(2,128)S(1)} %copy-done.3), custom_call_target="tpu_custom_call" | custom-call | tf_op jit(solution)/shard_map/strain_levels/pallas_call | solution.py:394
  16.9 2.0 %toeplitz_tiles.2.tiles_ref = bf16[8,19,128,128]{3,2,1,0:T(8,128)(2,1)S(1)} custom-call(f32[312,128]{1,0:T(8,128)S(1)} %strain_levels.1.flipped_ref), custom_call_target="tpu_custom_call" | custom-call | flops 159383552 | bytes 4980736 | tf_op jit(solution)/shard_map/toeplitz_tiles/pallas_call | solution.py:435
  18.9 0.0 copy-start
  18.9 2.3 %copy-done = bf16[8,19,128,128]{3,2,1,0:T(8,128)(2,1)} copy-done((bf16[8,19,128,128]{3,2,1,0:T(8,128)(2,1)}, bf16[8,19,128,128]{3,2,1,0:T(8,128)(2,1)S(1)}, u32[]{:S(2)}) %copy-start) | copy-done | bytes 4980760
  21.2 0.0 collective-permute-done.2
  21.2 1.6 %collective-permute-done.3 = f32[2,256,128]{2,1,0:T(8,128)S(1)} collective-permute-done((f32[2,256,128]{2,1,0:T(8,128)S(1)}, f32[2,256,128]{2,1,0:T(8,128)S(1)}, u32[]{:S(2)}, u32[]{:S(2)}) %collective-permute-start.3) | collective-permute-done | bytes 262176 | tf_op jit(solution)/shard_map/ppermute | solution.py:174
  22.9 2.1 %collective-permute-start.4 = (f32[256,128]{1,0:T(8,128)S(1)}, f32[256,128]{1,0:T(8,128)S(1)}, u32[]{:S(2)}, u32[]{:S(2)}) collective-permute-start(f32[256,128]{1,0:T(8,128)S(1)} %dynamic-slice_bitcast_fusion.1), channel_id=1, source_target_pairs={{0,16},{1,9},{2,18},{3,11},{4,20},{5,13},{6,22},{7,15},{8,24},{9,1... | collective-permute-start | bytes 393224 | tf_op jit(solution)/shard_map/ppermute | solution.py:174
  25.1 0.1 collective-permute-start.8
  25.2 2.2 %toeplitz_tiles.3.tiles_ref = bf16[8,16,128,128]{3,2,1,0:T(8,128)(2,1)S(1)} custom-call(f32[312,128]{1,0:T(8,128)S(1)} %strain_levels.1.flipped_ref), custom_call_target="tpu_custom_call" | custom-call | flops 134217728 | bytes 4194304 | tf_op jit(solution)/shard_map/toeplitz_tiles/pallas_call | solution.py:435
  27.4 0.6 collective-permute-done.4
  28.0 3.5 %collective-permute-start.5 = (f32[256,128]{1,0:T(8,128)S(1)}, f32[256,128]{1,0:T(8,128)S(1)}, u32[]{:S(2)}, u32[]{:S(2)}) collective-permute-start(f32[256,128]{1,0:T(8,128)S(1)} %bitcast_add_fusion.3), channel_id=1, source_target_pairs={{0,2},{1,5},{2,0},{3,7},{4,6},{5,1},{6,4},{7,3},{8,10},{9,13},{10,... | collective-permute-start | bytes 393224 | tf_op jit(solution)/shard_map/ppermute | solution.py:182
  31.5 0.0 collective-permute-done.8
  31.5 1.6 %collective-permute-start.9 = (f32[256,128]{1,0:T(8,128)S(1)}, f32[256,128]{1,0:T(8,128)S(1)}, u32[]{:S(2)}, u32[]{:S(2)}) collective-permute-start(f32[256,128]{1,0:T(8,128)S(1)} %bitcast_add_fusion.2), channel_id=1, source_target_pairs={{0,2},{1,5},{2,0},{3,7},{4,6},{5,1},{6,4},{7,3},{8,10},{9,13},{10,... | collective-permute-start | bytes 393224 | tf_op jit(solution)/shard_map/ppermute | solution.py:182
  33.1 1.9 %collective-permute-done.5 = f32[256,128]{1,0:T(8,128)S(1)} collective-permute-done((f32[256,128]{1,0:T(8,128)S(1)}, f32[256,128]{1,0:T(8,128)S(1)}, u32[]{:S(2)}, u32[]{:S(2)}) %collective-permute-start.5) | collective-permute-done | bytes 131104 | tf_op jit(solution)/shard_map/ppermute | solution.py:182
  35.0 3.2 %collective-permute-start.6 = (f32[256,128]{1,0:T(8,128)S(1)}, f32[256,128]{1,0:T(8,128)S(1)}, u32[]{:S(2)}, u32[]{:S(2)}) collective-permute-start(f32[256,128]{1,0:T(8,128)S(1)} %add.92), channel_id=1, source_target_pairs={{0,4},{1,3},{2,6},{3,1},{4,0},{5,7},{6,2},{7,5},{8,12},{9,11},{10,... | collective-permute-start | bytes 393224 | tf_op jit(solution)/shard_map/ppermute | solution.py:182
  38.2 0.0 collective-permute-done.9
  38.2 2.8 %collective-permute-start.10 = (f32[256,128]{1,0:T(8,128)S(1)}, f32[256,128]{1,0:T(8,128)S(1)}, u32[]{:S(2)}, u32[]{:S(2)}) collective-permute-start(f32[256,128]{1,0:T(8,128)S(1)} %add.95), channel_id=1, source_target_pairs={{0,4},{1,3},{2,6},{3,1},{4,0},{5,7},{6,2},{7,5},{8,12},{9,11},{10,... | collective-permute-start | bytes 393224 | tf_op jit(solution)/shard_map/ppermute | solution.py:182
  41.0 0.2 collective-permute-done.6
  41.3 0.1 collective-permute-start.7
  41.4 3.1 %collective-permute-done.10 = f32[256,128]{1,0:T(8,128)S(1)} collective-permute-done((f32[256,128]{1,0:T(8,128)S(1)}, f32[256,128]{1,0:T(8,128)S(1)}, u32[]{:S(2)}, u32[]{:S(2)}) %collective-permute-start.10) | collective-permute-done | bytes 131104 | tf_op jit(solution)/shard_map/ppermute | solution.py:182
  44.5 0.1 collective-permute-start.11
  44.6 0.0 collective-permute-done.7.other_ref
  44.6 4.6 %basis_first.1 = (f32[512,128]{1,0:T(8,128)S(1)}, f32[1,128]{1,0:T(1,128)S(1)}) custom-call(f32[256,128]{1,0:T(8,128)S(1)} %add.93.mine_ref, f32[256,128]{1,0:T(8,128)S(1)} %collective-permute-done.7.other_ref), custom_call_target="tpu_custom_call" | custom-call | tf_op jit(solution)/shard_map/basis_first/pallas_call | solution.py:289
  49.2 0.0 collective-permute-done.11.other_ref
  49.2 5.6 %basis_second.1 = (bf16[512,256]{1,0:T(8,128)(2,1)S(1)}, bf16[256,256]{1,0:T(8,128)(2,1)S(1)}, bf16[640,256]{1,0:T(8,128)(2,1)S(1)}, f32[1,256]{1,0:T(1,128)}) custom-call(f32[512,128]{1,0:T(8,128)S(1)} %get-tuple-element.47.first_ref, f32[1,128]{1,0:T(1,128)S(1)} %get-tuple-element.48.first_spectrum_ref, f32[256,128]{1,0:T(8,128)S(1)} %add.96.mine_ref, ...), custom_call_target="tpu_custom_call" | custom-call | tf_op jit(solution)/shard_map/basis_second/pallas_call | solution.py:329
  54.8 2.4 %collective-permute-start.13 = (bf16[256,256]{1,0:T(8,128)(2,1)S(1)}, bf16[256,256]{1,0:T(8,128)(2,1)S(1)}, u32[]{:S(2)}, u32[]{:S(2)}) collective-permute-start(bf16[256,256]{1,0:T(8,128)(2,1)S(1)} %get-tuple-element.58), channel_id=1, source_target_pairs={{0,24},{1,25},{2,26},{3,27},{4,28},{5,29},{6,30},{7,31},{8,16},{9,... | collective-permute-start | bytes 393224 | tf_op jit(solution)/shard_map/ppermute | solution.py:174
  57.3 0.5 collective-permute-start.12
  57.8 5.6 %filter_levels.2 = bf16[1,2,8192,256]{3,2,1,0:T(8,128)(2,1)} custom-call(bf16[8,19,128,128]{3,2,1,0:T(8,128)(2,1)S(1)} %copy-done.1, bf16[512,256]{1,0:T(8,128)(2,1)S(1)} %get-tuple-element.56.taps_ref.own_ref), custom_call_target="tpu_custom_call" | custom-call | flops 4294967296 | bytes 13369344 | tf_op jit(solution)/shard_map/filter_levels/pallas_call | solution.py:497
  63.4 0.0 copy-start.2
  63.4 0.0 copy-start.4
  63.4 0.0 collective-permute-done.13
  63.4 1.1 %collective-permute-done.12 = bf16[512,256]{1,0:T(8,128)(2,1)S(1)} collective-permute-done((bf16[512,256]{1,0:T(8,128)(2,1)S(1)}, bf16[512,256]{1,0:T(8,128)(2,1)S(1)}, u32[]{:S(2)}, u32[]{:S(2)}) %collective-permute-start.12) | collective-permute-done | bytes 262176 | tf_op jit(solution)/shard_map/ppermute | solution.py:174
  64.5 0.1 collective-permute-start.14
  64.6 3.9 %filter_levels.3 = (bf16[1,2,4096,256]{3,2,1,0:T(8,128)(2,1)}, bf16[1,2,2048,256]{3,2,1,0:T(8,128)(2,1)}, bf16[1,2,1024,256]{3,2,1,0:T(8,128)(2,1)}, bf16[1,2,512,256]{3,2,1,0:T(8,128)(2,1)}) custom-call(bf16[8,16,128,128]{3,2,1,0:T(8,128)(2,1)S(1)} %toeplitz_tiles.3.tiles_ref, bf16[640,256]{1,0:T(8,128)(2,1)S(1)} %get-tuple-element.66.taps_ref), custom_call_target="tpu_custom_call" | custom-call | flops 1543503872 | bytes 12058624 | tf_op jit(solution)/shard_map/filter_levels/pallas_call | solution.py:497
  68.6 0.0 collective-permute-done.14.other_ref
  68.6 2.6 %mixing.1 = bf16[1024,256]{1,0:T(8,128)(2,1)} custom-call(s32[1,1024]{1,0:T(1,128)S(1)} %bitcast.19, bf16[1024,512]{1,0:T(8,128)(2,1)S(1)} %copy-done.2, bf16[512,256]{1,0:T(8,128)(2,1)S(1)} %get-tuple-element.56.taps_ref.own_ref, bf16[768,256]{1,0:T(8,128)(2,1)S(1)} %constant_dynamic-update-slice_fusion.mine_ref, ...), custom_call_target="tpu_custom_call" | custom-call | tf_op jit(solution)/shard_map/mixing/pallas_call | solution.py:537
  (18 shorter events, 0.3 us)
Async XLA Ops:
  0.6 15.2 %copy-start.3 = (f32[2,8192]{1,0:T(2,128)S(1)}, f32[2,8192]{1,0:T(2,128)}, u32[]{:S(2)}) copy-start(f32[2,8192]{1,0:T(2,128)} %strain_ref.1) | copy-start | bytes 196612
  8.1 4.5 %collective-permute-start = (f32[2,2,2,256,128]{4,3,2,1,0:T(8,128)}, f32[2,2,2,256,128]{4,3,2,1,0:T(8,128)S(1)}, u32[]{:S(2)}, u32[]{:S(2)}) collective-permute-start(f32[2,2,2,256,128]{4,3,2,1,0:T(8,128)} %get-tuple-element.42), channel_id=1, source_target_pairs={{0,1},{1,0},{2,3},{3,2},{4,5},{5,4},{6,7},{7,6},{8,9},{9,8},{10,11... | collective-permute-start | bytes 3145736 | tf_op jit(solution)/shard_map/ppermute | solution.py:178
  9.3 3.3 %collective-permute-start.1 = (f32[2,2048]{1,0:T(2,128)S(1)}, f32[2,2048]{1,0:T(2,128)S(1)}, u32[]{:S(2)}, u32[]{:S(2)}) collective-permute-start(f32[2,2048]{1,0:T(2,128)S(1)} %slice.20), channel_id=1, source_target_pairs={{0,1},{1,2},{2,3},{3,4},{4,5},{5,6},{6,7},{8,9},{9,10},{10,11},{11... | collective-permute-start | bytes 49160 | tf_op jit(solution)/shard_map/ppermute | solution.py:564
  12.7 8.5 %collective-permute-start.2 = (f32[2,256,128]{2,1,0:T(8,128)S(1)}, f32[2,256,128]{2,1,0:T(8,128)S(1)}, u32[]{:S(2)}, u32[]{:S(2)}) collective-permute-start(f32[2,256,128]{2,1,0:T(8,128)S(1)} %add_bitcast_fusion.1), channel_id=1, source_target_pairs={{0,8},{1,17},{2,10},{3,19},{4,12},{5,21},{6,14},{7,23},{8,0},{9,25... | collective-permute-start | bytes 786440 | tf_op jit(solution)/shard_map/ppermute | solution.py:174
  15.7 7.1 %collective-permute-start.3 = (f32[2,256,128]{2,1,0:T(8,128)S(1)}, f32[2,256,128]{2,1,0:T(8,128)S(1)}, u32[]{:S(2)}, u32[]{:S(2)}) collective-permute-start(f32[2,256,128]{2,1,0:T(8,128)S(1)} %add_bitcast_fusion), channel_id=1, source_target_pairs={{0,8},{1,17},{2,10},{3,19},{4,12},{5,21},{6,14},{7,23},{8,0},{9,25... | collective-permute-start | bytes 786440 | tf_op jit(solution)/shard_map/ppermute | solution.py:174
  18.9 2.3 %copy-start = (bf16[8,19,128,128]{3,2,1,0:T(8,128)(2,1)}, bf16[8,19,128,128]{3,2,1,0:T(8,128)(2,1)S(1)}, u32[]{:S(2)}) copy-start(bf16[8,19,128,128]{3,2,1,0:T(8,128)(2,1)S(1)} %toeplitz_tiles.2.tiles_ref) | copy-start | bytes 14942212
  22.9 5.1 %collective-permute-start.4 = (f32[256,128]{1,0:T(8,128)S(1)}, f32[256,128]{1,0:T(8,128)S(1)}, u32[]{:S(2)}, u32[]{:S(2)}) collective-permute-start(f32[256,128]{1,0:T(8,128)S(1)} %dynamic-slice_bitcast_fusion.1), channel_id=1, source_target_pairs={{0,16},{1,9},{2,18},{3,11},{4,20},{5,13},{6,22},{7,15},{8,24},{9,1... | collective-permute-start | bytes 393224 | tf_op jit(solution)/shard_map/ppermute | solution.py:174
  25.0 32.8 %copy-start.1 = (bf16[8,19,128,128]{3,2,1,0:T(8,128)(2,1)S(1)}, bf16[8,19,128,128]{3,2,1,0:T(8,128)(2,1)}, u32[]{:S(2)}) copy-start(bf16[8,19,128,128]{3,2,1,0:T(8,128)(2,1)} %copy-done) | copy-start | bytes 14942212
  25.1 6.4 %collective-permute-start.8 = (f32[256,128]{1,0:T(8,128)S(1)}, f32[256,128]{1,0:T(8,128)S(1)}, u32[]{:S(2)}, u32[]{:S(2)}) collective-permute-start(f32[256,128]{1,0:T(8,128)S(1)} %dynamic-slice_bitcast_fusion), channel_id=1, source_target_pairs={{0,16},{1,9},{2,18},{3,11},{4,20},{5,13},{6,22},{7,15},{8,24},{9,1... | collective-permute-start | bytes 393224 | tf_op jit(solution)/shard_map/ppermute | solution.py:174
  28.0 7.0 %collective-permute-start.5 = (f32[256,128]{1,0:T(8,128)S(1)}, f32[256,128]{1,0:T(8,128)S(1)}, u32[]{:S(2)}, u32[]{:S(2)}) collective-permute-start(f32[256,128]{1,0:T(8,128)S(1)} %bitcast_add_fusion.3), channel_id=1, source_target_pairs={{0,2},{1,5},{2,0},{3,7},{4,6},{5,1},{6,4},{7,3},{8,10},{9,13},{10,... | collective-permute-start | bytes 393224 | tf_op jit(solution)/shard_map/ppermute | solution.py:182
  31.5 6.7 %collective-permute-start.9 = (f32[256,128]{1,0:T(8,128)S(1)}, f32[256,128]{1,0:T(8,128)S(1)}, u32[]{:S(2)}, u32[]{:S(2)}) collective-permute-start(f32[256,128]{1,0:T(8,128)S(1)} %bitcast_add_fusion.2), channel_id=1, source_target_pairs={{0,2},{1,5},{2,0},{3,7},{4,6},{5,1},{6,4},{7,3},{8,10},{9,13},{10,... | collective-permute-start | bytes 393224 | tf_op jit(solution)/shard_map/ppermute | solution.py:182
  35.0 6.3 %collective-permute-start.6 = (f32[256,128]{1,0:T(8,128)S(1)}, f32[256,128]{1,0:T(8,128)S(1)}, u32[]{:S(2)}, u32[]{:S(2)}) collective-permute-start(f32[256,128]{1,0:T(8,128)S(1)} %add.92), channel_id=1, source_target_pairs={{0,4},{1,3},{2,6},{3,1},{4,0},{5,7},{6,2},{7,5},{8,12},{9,11},{10,... | collective-permute-start | bytes 393224 | tf_op jit(solution)/shard_map/ppermute | solution.py:182
  38.2 6.2 %collective-permute-start.10 = (f32[256,128]{1,0:T(8,128)S(1)}, f32[256,128]{1,0:T(8,128)S(1)}, u32[]{:S(2)}, u32[]{:S(2)}) collective-permute-start(f32[256,128]{1,0:T(8,128)S(1)} %add.95), channel_id=1, source_target_pairs={{0,4},{1,3},{2,6},{3,1},{4,0},{5,7},{6,2},{7,5},{8,12},{9,11},{10,... | collective-permute-start | bytes 393224 | tf_op jit(solution)/shard_map/ppermute | solution.py:182
  41.3 3.3 %collective-permute-start.7 = (f32[256,128]{1,0:T(8,128)S(1)}, f32[256,128]{1,0:T(8,128)S(1)}, u32[]{:S(2)}, u32[]{:S(2)}) collective-permute-start(f32[256,128]{1,0:T(8,128)S(1)} %add.93.mine_ref), channel_id=1, source_target_pairs={{0,1},{1,0},{2,3},{3,2},{4,5},{5,4},{6,7},{7,6},{8,9},{9,8},{10,11... | collective-permute-start | bytes 393224 | tf_op jit(solution)/shard_map/ppermute | solution.py:178
  44.5 4.7 %collective-permute-start.11 = (f32[256,128]{1,0:T(8,128)S(1)}, f32[256,128]{1,0:T(8,128)S(1)}, u32[]{:S(2)}, u32[]{:S(2)}) collective-permute-start(f32[256,128]{1,0:T(8,128)S(1)} %add.96.mine_ref), channel_id=1, source_target_pairs={{0,1},{1,0},{2,3},{3,2},{4,5},{5,4},{6,7},{7,6},{8,9},{9,8},{10,11... | collective-permute-start | bytes 393224 | tf_op jit(solution)/shard_map/ppermute | solution.py:178
  54.8 8.6 %collective-permute-start.13 = (bf16[256,256]{1,0:T(8,128)(2,1)S(1)}, bf16[256,256]{1,0:T(8,128)(2,1)S(1)}, u32[]{:S(2)}, u32[]{:S(2)}) collective-permute-start(bf16[256,256]{1,0:T(8,128)(2,1)S(1)} %get-tuple-element.58), channel_id=1, source_target_pairs={{0,24},{1,25},{2,26},{3,27},{4,28},{5,29},{6,30},{7,31},{8,16},{9,... | collective-permute-start | bytes 393224 | tf_op jit(solution)/shard_map/ppermute | solution.py:174
  57.3 7.2 %collective-permute-start.12 = (bf16[512,256]{1,0:T(8,128)(2,1)S(1)}, bf16[512,256]{1,0:T(8,128)(2,1)S(1)}, u32[]{:S(2)}, u32[]{:S(2)}) collective-permute-start(bf16[512,256]{1,0:T(8,128)(2,1)S(1)} %get-tuple-element.56.taps_ref.own_ref), channel_id=1, source_target_pairs={{0,8},{1,17},{2,10},{3,19},{4,12},{5,21},{6,14},{7,23},{8,0},{9,25... | collective-permute-start | bytes 786440 | tf_op jit(solution)/shard_map/ppermute | solution.py:174
  63.4 5.2 %copy-start.2 = (bf16[1024,512]{1,0:T(8,128)(2,1)S(1)}, bf16[1024,512]{1,0:T(8,128)(2,1)}, u32[]{:S(2)}) copy-start(bf16[1024,512]{1,0:T(8,128)(2,1)} %get-tuple-element.39.white_ref) | copy-start | bytes 3145732
  63.4 5.2 %copy-start.4 = (s32[1024,1]{0,1:T(1,128)S(1)}, s32[1024,1]{0,1:T(1,128)}, u32[]{:S(2)}) copy-start(s32[1024,1]{0,1:T(1,128)} %param.7) | copy-start | bytes 12292
  64.5 4.0 %collective-permute-start.14 = (bf16[768,256]{1,0:T(8,128)(2,1)S(1)}, bf16[768,256]{1,0:T(8,128)(2,1)S(1)}, u32[]{:S(2)}, u32[]{:S(2)}) collective-permute-start(bf16[768,256]{1,0:T(8,128)(2,1)S(1)} %constant_dynamic-update-slice_fusion.mine_ref), channel_id=1, source_target_pairs={{0,1},{1,0},{2,3},{3,2},{4,5},{5,4},{6,7},{7,6},{8,9},{9,8},{10,11... | collective-permute-start | bytes 1179656 | tf_op jit(solution)/shard_map/ppermute | solution.py:178

commit v3 on v2

--- a/solution.py
+++ b/solution.py
@@ -185,7 +185,6 @@
 def reduce_products(keep, send, bins, grp, beside):
     keep, done = beside[0](keep, ())
     came = flip_core(send, grp)
-    came, *done = lax.optimization_barrier((came, *done))
     came, done = beside[1](came, done)
     here = lax.axis_index("bin")
     core = lax.axis_index("grp") % 2
@@ -197,13 +196,13 @@
         arrived = [move(x) for x in leaving]
         return [x + y for x, y in zip(held, arrived)]
 
-    total = stage(
-        [pick(keep[i], one) + pick(came[i], one) for i in pieces],
-        [pick(keep[i], 1 - one) + pick(came[i], 1 - one) for i in pieces],
-        lambda x: flip_bin(x, (1, 2), bins, grp),
-    )
-    *total, done_0, done_1 = lax.optimization_barrier((*total, *done))
-    total[-1], done = beside[2](total[-1], (done_0, done_1))
+    def side(which):
+        return jnp.stack([pick(keep[i], which) + pick(came[i], which) for i in pieces])
+
+    arrived = flip_bin(side(1 - one), (1, 2), bins, grp)
+    arrived, *done = lax.optimization_barrier((arrived, *done))
+    total = [pick(keep[i], one) + pick(came[i], one) + arrived[i] for i in pieces]
+    total[-1], done = beside[2](total[-1], done)
     mine = stage(
         [pick(x, two) for x in total],
         [pick(x, 1 - two) for x in total],
@@ -211,8 +210,11 @@
     )
     bits = [1 << i for i in range((grp // 2).bit_length() - 1)]
     mine[-1], *done = lax.optimization_barrier((mine[-1], *done))
+    mine[-1], done = beside[3](mine[-1], done)
     for step, bit in enumerate(bits):
         mine = stage(mine, mine, lambda x: flip_chip(x, (bit, bits[-1 - step]), grp))
+        if step == 0:
+            mine[-1], *done = lax.optimization_barrier((mine[-1], *done))
     return mine, [flip_core(x, grp) for x in mine], done
 
 
@@ -220,19 +222,21 @@
     finished = []
     size = state.shape[0]
     head = iota((SUBLANES, size), 0)
+
+    def spread_column(rows, column):
+        return jnp.broadcast_to(rows[:, column : column + 1], rows.shape)
+
+    tops = [spread_column(state[:SUBLANES], k) for k in range(SUBLANES)]
     for start in range(0, size, SUBLANES):
-        lane = iota(state.shape, 1)
-        columns = [
-            jnp.broadcast_to(state[:, start + k : start + k + 1], state.shape)
-            for k in range(SUBLANES)
-        ]
-        state = jnp.where((lane >= start) & (lane < start + SUBLANES), f32(0.0), state)
+        after = start + SUBLANES
         eye = iota((SUBLANES, size), 1) == head + start
-        top = jnp.where(eye, f32(1.0), state[:SUBLANES])
-        rest = state[SUBLANES:]
+        top, rest = state[:SUBLANES], state[SUBLANES:]
         more = rest.shape[0] > 0
-        tops = [column[:SUBLANES] for column in columns]
-        rests = [column[SUBLANES:] for column in columns]
+        rests = [spread_column(rest, start + k) for k in range(SUBLANES)] if more else []
+        nexts = [spread_column(rest[:SUBLANES], after + k) for k in range(SUBLANES)] if more else []
+        top = jnp.where(eye, f32(1.0), jnp.where(in_lanes(top, start, after), f32(0.0), top))
+        if more:
+            rest = jnp.where(in_lanes(rest, start, after), f32(0.0), rest)
         pivots = jnp.zeros((SUBLANES, size), f32)
         for k in range(SUBLANES):
             pivot = tops[k][k : k + 1]
@@ -244,15 +248,23 @@
                 tops[j] = tops[j] - (below * across) * inverse
                 if more:
                     rests[j] = rests[j] - factor * across
+            if more:
+                for j in range(SUBLANES):
+                    nexts[j] = nexts[j] - factor[:SUBLANES] * rests[k][j : j + 1]
             across = top[k : k + 1]
             top = top - (below * across) * inverse
             if more:
                 rest = rest - factor * across
             pivots = jnp.where(head == k, pivot, pivots)
         finished.append(top * lax.rsqrt(pivots))
-        state = rest
+        state, tops = rest, nexts
     inverse = jnp.concatenate(finished, axis=0)
     return jnp.where(iota((size, size), 0) >= iota((size, size), 1), inverse, f32(0.0))
+
+
+def in_lanes(x, first, end):
+    lane = iota(x.shape, 1)
+    return (lane >= first) & (lane < end)
 
 
 def joined_rows(mine_ref, other_ref, product_ref):
@@ -447,7 +459,7 @@
     )(flipped)
 
 
-def filter_body(blocks, chunks, unroll, tiles_ref, taps_ref, *refs):
+def filter_body(blocks, chunks, tiles_ref, taps_ref, *refs):
     count = len(blocks)
     out_refs, held_refs = refs[:count], refs[count : 2 * count]
     here_ref, out_sem = tiles_ref, refs[2 * count]
@@ -480,22 +492,19 @@
             at += rows // LANES + b - 1
             tap_at += b * LANES
 
-    if unroll:
-        for step in range(steps):
-            work(step)
-    else:
-        pl.loop(0, steps)(work)
+    for step in range(steps):
+        work(step)
     for step in range(steps):
         for r in range(count):
             give(step, r).wait()
 
 
-def filter_levels(tiles, taps, lengths, blocks, detectors, chunks, unroll=True):
+def filter_levels(tiles, taps, lengths, blocks, detectors, chunks):
     rank = taps.shape[1]
     steps = tiles.shape[0]
     anywhere = pl.BlockSpec(memory_space=pl.ANY)
     return pl.pallas_call(
-        functools.partial(filter_body, blocks, chunks, unroll),
+        functools.partial(filter_body, blocks, chunks),
         out_shape=[jax.ShapeDtypeStruct((1, detectors, n, rank), bf16) for n in lengths],
         in_specs=[pl.BlockSpec(memory_space=pltpu.VMEM)] * 2,
         out_specs=[anywhere] * len(lengths),
@@ -511,24 +520,40 @@
     )(tiles, taps)
 
 
-def mixing_body(bins, grp, owner_ref, white_ref, own_ref, mine_ref, other_ref, out_ref, bases_ref):
+def mixing_body(bins, grp, owner_ref, white_ref, own_ref, mine_ref, other_ref, out_hbm, bases_ref, out_ref,
+                sem):
     rows, width = white_ref.shape
-    rank = own_ref.shape[1]
     half = width // 2
     core, here = lax.axis_index("grp") % 2, lax.axis_index("bin")
-    bases_ref[0] = own_ref[...]
-    bases_ref[1 + core] = mine_ref[:width]
-    bases_ref[2 - core] = other_ref[:width]
-    bases_ref[3, pl.ds(pl.multiple_of(core * half, half), half), :] = mine_ref[width:]
-    bases_ref[3, pl.ds(pl.multiple_of((1 - core) * half, half), half), :] = other_ref[width:]
-    mask = spread((owner_ref[...] // grp) ^ here, rows, bins, rank)
-    white = white_ref[...]
-    total = None
-    for m in range(bins):
-        chosen = mask[:, m * rank : (m + 1) * rank] > 0.5
-        term = jnp.where(chosen, dot(white, bases_ref[m]), f32(0.0))
-        total = term if total is None else total + term
-    out_ref[...] = total.astype(bf16)
+
+    def place(row, count):
+        return pl.ds(pl.multiple_of(row, count), count)
+
+    bases_ref[:width] = own_ref[...]
+    bases_ref[place((1 + core) * width, width), :] = mine_ref[:width]
+    bases_ref[place((2 - core) * width, width), :] = other_ref[:width]
+    bases_ref[place(3 * width + core * half, half), :] = mine_ref[width:]
+    bases_ref[place(3 * width + (1 - core) * half, half), :] = other_ref[width:]
+    mask = spread((owner_ref[...] // grp) ^ here, rows, bins, LANES).astype(bf16)
+    pieces = 4
+    piece = rows // pieces
+    given = []
+    for i in range(pieces):
+        at = slice(i * piece, (i + 1) * piece)
+        white = white_ref[at, :]
+        masked = jnp.concatenate(
+            [
+                white * jnp.concatenate([mask[at, m * LANES : (m + 1) * LANES]] * (width // LANES), axis=1)
+                for m in range(bins)
+            ],
+            axis=1,
+        )
+        out_ref[at, :] = dot(masked, bases_ref[...]).astype(bf16)
+        rows_at = pl.ds(i * piece, piece)
+        given.append(pltpu.make_async_copy(out_ref.at[rows_at], out_hbm.at[rows_at], sem.at[i]))
+        given[-1].start()
+    for copy in given:
+        copy.wait()
 
 
 def mix(owner, white, own, mine, other, bins, grp):
@@ -537,7 +562,13 @@
     return pl.pallas_call(
         functools.partial(mixing_body, bins, grp),
         out_shape=jax.ShapeDtypeStruct((rows, rank), bf16),
-        scratch_shapes=[pltpu.VMEM((bins, width, rank), bf16)],
+        in_specs=[pl.BlockSpec(memory_space=pltpu.VMEM)] * 5,
+        out_specs=pl.BlockSpec(memory_space=pl.ANY),
+        scratch_shapes=[
+            pltpu.VMEM((bins * width, rank), bf16),
+            pltpu.VMEM((rows, rank), bf16),
+            pltpu.SemaphoreType.DMA((4,)),
+        ],
         compiler_params=params(14),
         name="mixing",
     )(owner, white, own, mine, other)
@@ -564,20 +595,19 @@
         history = lax.ppermute(here[:, -reach:], "grp", [(i, i + 1) for i in range(grp - 1)])
         return x, (history,)
 
-    def fine(x, done):
-        x, history = lax.optimization_barrier((x, *done))
-        flipped = flipped_levels(history, strain, levels)
-        return x, (flipped, tiles_of(flipped, (0,)))
-
-    def coarse(x, done):
-        x, flipped, tiles = lax.optimization_barrier((x, *done))
-        return x, (tiles, tiles_of(flipped, tuple(range(1, levels))))
-
-    def tiles_of(flipped, wanted):
-        return make_tiles(flipped, total, wanted, levels, blocks, detectors, chunks)
-
-    mine, other, (tiles_fine, tiles_coarse) = reduce_products(
-        keep, send, bins, grp, (before, fine, coarse)
+    def lines(x, done):
+        return x, (flipped_levels(*done, strain, levels),)
+
+    def tiles_of(wanted):
+        def work(x, done):
+            x, flipped, *rest = lax.optimization_barrier((x, *done))
+            tiles = make_tiles(flipped, total, wanted, levels, blocks, detectors, chunks)
+            return x, (flipped, *rest, tiles)
+
+        return work
+
+    mine, other, (_, tiles_coarse, tiles_fine) = reduce_products(
+        keep, send, bins, grp, (before, lines, tiles_of(tuple(range(1, levels))), tiles_of((0,)))
     )
     own, part, taps, spectrum = find_basis(
         mine, other, sum(blocks[1:]) * LANES, rows * grp * math.sqrt(width)

time: 71.9 us -> 69.3 us (0.964)
  waiting for transfers between devices: 8.61 us -> 11.9 us
  local copies, waits for them, and re-layouts: 4.41 us -> 1.41 us
  Pallas kernels: 35 us -> 32.8 us
    unnamed x11 -> x7, local copies, waits for them, and re-layouts: 2.3 us -> 0.03 us
    ppermute x6 -> x5, waiting for transfers between devices: 3.34 us -> 5.42 us  [flip_bin(): return lax.ppermute(x, ('bin', 'grp'), pairs)]
    ppermute x4, starting transfers between devices: 11 us -> 9.35 us  [flip_chip(): lax.ppermute(x, 'grp', [(i, i ^ 2 * bits[i % 2]) for i in range(grp)])]
    ppermute x6 -> x5, starting transfers between devices: 8.29 us -> 9.68 us  [flip_bin(): return lax.ppermute(x, ('bin', 'grp'), pairs)]
    ppermute x4, waiting for transfers between devices: 0.01 us -> 1.23 us  [flip_core(): return lax.ppermute(x, 'grp', [(i, i ^ 1) for i in range(grp)])]
    pallas_call x1, Pallas kernels: 4.59 us -> 3.65 us  [first_piece(): pl.pallas_call(functools.partial(piece_body, scale_down), out_shape=(jax....]
    ppermute x1, waiting for transfers between devices: 0.01 us -> 0.81 us  [before(): lax.ppermute(here[:, -reach:], 'grp', [(i, i + 1) for i in range(grp - 1)])]
    ppermute x4, waiting for transfers between devices: 5.26 us -> 4.47 us  [flip_chip(): lax.ppermute(x, 'grp', [(i, i ^ 2 * bits[i % 2]) for i in range(grp)])]
  transfers between devices with their start and end apart: 15 -> 14, of which waited for: 6 -> 8; matrix products, arithmetic and copies ran while one was open for 3% -> 2% of each run, Pallas kernels for 27% -> 26%
where the time goes in v3:
time: 69.3 us; the launch traced here: 69 us
  Pallas kernels  32.8 us (47%)
  starting transfers between devices  21.5 us (31%)
  waiting for transfers between devices  11.9 us (17%)
  local copies, waits for them, and re-layouts  1.41 us (2%)
  between operations  1.05 us (2%)
    ppermute x5, starting transfers between devices, flip_bin(): return lax.ppermute(x, ('bin', 'grp'), pairs)  9.68 us
    ppermute x4, starting transfers between devices, flip_chip(): lax.ppermute(x, 'grp', [(i, i ^ 2 * bits[i % 2]) for i in range(grp)])  9.35 us
    pallas_call x2, Pallas kernels, filter_levels(): pl.pallas_call(functools.partial(filter_body, blocks, chunks), out_shape=...  9.24 us
    pallas_call x1, Pallas kernels, front(): pl.pallas_call(functools.partial(front_body, bins, grp), out_shape=(jax.S...  7.4 us
    ppermute x5, waiting for transfers between devices, flip_bin(): return lax.ppermute(x, ('bin', 'grp'), pairs)  5.42 us
    pallas_call x1, Pallas kernels, find_basis(): pl.pallas_call(functools.partial(basis_body, scale_down), out_shape=(jax....  4.86 us
    ppermute x4, waiting for transfers between devices, flip_chip(): lax.ppermute(x, 'grp', [(i, i ^ 2 * bits[i % 2]) for i in range(grp)])  4.47 us
    pallas_call x2, Pallas kernels, make_tiles(): pl.pallas_call(functools.partial(tiles_body, wanted, total, levels, block...  4.23 us
  transfers between devices with their start and end apart: 14, of which 8 were waited for; matrix products, arithmetic and copies ran while one was open for 2% of the time, Pallas kernels for 26%

profile of v3, /device:TPU:0, one launch (start us, length us, event | category | flops | bytes accessed | tf_op | source)
XLA Modules:
  0.0 69.0 jit_solution(16642816174544676554)
XLA Ops:
  0.6 0.0 copy-start.1
  0.6 7.4 %whiten_products.1 = (bf16[1024,512]{1,0:T(8,128)(2,1)}, f32[2,2,2,256,128]{4,3,2,1,0:T(8,128)}, f32[2,2,2,256,128]{4,3,2,1,0:T(8,128)}) custom-call(s32[1,1024]{1,0:T(1,128)} %bitcast.22, s32[1,1024]{1,0:T(1,128)} %bitcast.24, f32[5,512]{1,0:T(8,128)} %gains_hbm.1, bf16[1024,512]{1,0:T(8,128)(2,1)} %templates_hbm.1, f32[512,256]{1,0:T(8,128)} %sketch_hbm.1), custom_call_target="tpu_custom_call" | custom-call | tf_op jit(solution)/shard_map/whiten_products/pallas_call | solution.py:141
  8.1 0.5 collective-permute-start
  8.6 1.3 %fusion = (f32[1,2,2,256,128]{4,3,2,1,0:T(8,128)S(1)}, f32[1,2,2,256,128]{4,3,2,1,0:T(8,128)S(1)}) fusion(f32[2,2,2,256,128]{4,3,2,1,0:T(8,128)} %get-tuple-element.39), kind=kLoop, calls=%fused_computation.11 | loop fusion | bytes 2097152 | tf_op jit(solution)/shard_map/slice | solution.py:204
  9.8 1.2 %collective-permute-done = f32[2,2,2,256,128]{4,3,2,1,0:T(8,128)S(1)} collective-permute-done((f32[2,2,2,256,128]{4,3,2,1,0:T(8,128)}, f32[2,2,2,256,128]{4,3,2,1,0:T(8,128)S(1)}, u32[]{:S(2)}, u32[]{:S(2)}) %collective-permute-start) | collective-permute-done | bytes 1048608 | tf_op jit(solution)/shard_map/ppermute | solution.py:178
  11.1 0.1 fusion.1
  11.1 0.1 add_bitcast_fusion
  11.2 2.9 %collective-permute-start.1 = (f32[2,2,256,128]{3,2,1,0:T(8,128)S(1)}, f32[2,2,256,128]{3,2,1,0:T(8,128)S(1)}, u32[]{:S(2)}, u32[]{:S(2)}) collective-permute-start(f32[2,2,256,128]{3,2,1,0:T(8,128)S(1)} %pad_maximum_fusion), channel_id=1, source_target_pairs={{0,8},{1,17},{2,10},{3,19},{4,12},{5,21},{6,14},{7,23},{8,0},{9,25... | collective-permute-start | bytes 1572872 | tf_op jit(solution)/shard_map/ppermute | solution.py:174
  14.2 0.0 copy-done.1
  14.2 1.8 %collective-permute-start.2 = (f32[2,2048]{1,0:T(2,128)S(1)}, f32[2,2048]{1,0:T(2,128)S(1)}, u32[]{:S(2)}, u32[]{:S(2)}) collective-permute-start(f32[2,2048]{1,0:T(2,128)S(1)} %slice.29), channel_id=1, source_target_pairs={{0,1},{1,2},{2,3},{3,4},{4,5},{5,6},{6,7},{8,9},{9,10},{10,11},{11... | collective-permute-start | bytes 49160 | tf_op jit(solution)/shard_map/ppermute | solution.py:595
  16.0 0.8 %collective-permute-done.2.history_ref = f32[2,2048]{1,0:T(2,128)S(1)} collective-permute-done((f32[2,2048]{1,0:T(2,128)S(1)}, f32[2,2048]{1,0:T(2,128)S(1)}, u32[]{:S(2)}, u32[]{:S(2)}) %collective-permute-start.2) | collective-permute-done | bytes 16416 | tf_op jit(solution)/shard_map/ppermute | solution.py:595
  16.8 1.0 %strain_levels.1.flipped_ref = f32[312,128]{1,0:T(8,128)S(1)} custom-call(f32[2,2048]{1,0:T(2,128)S(1)} %collective-permute-done.2.history_ref, f32[2,8192]{1,0:T(2,128)S(1)} %copy-done.1), custom_call_target="tpu_custom_call" | custom-call | tf_op jit(solution)/shard_map/strain_levels/pallas_call | solution.py:406
  17.8 3.5 %collective-permute-done.1 = f32[2,2,256,128]{3,2,1,0:T(8,128)S(1)} collective-permute-done((f32[2,2,256,128]{3,2,1,0:T(8,128)S(1)}, f32[2,2,256,128]{3,2,1,0:T(8,128)S(1)}, u32[]{:S(2)}, u32[]{:S(2)}) %collective-permute-start.1) | collective-permute-done | bytes 524320 | tf_op jit(solution)/shard_map/ppermute | solution.py:174
  21.3 0.1 bitcast_add_fusion
  21.4 2.1 %collective-permute-start.3 = (f32[256,128]{1,0:T(8,128)S(1)}, f32[256,128]{1,0:T(8,128)S(1)}, u32[]{:S(2)}, u32[]{:S(2)}) collective-permute-start(f32[256,128]{1,0:T(8,128)S(1)} %dynamic-slice_bitcast_fusion.1), channel_id=1, source_target_pairs={{0,16},{1,9},{2,18},{3,11},{4,20},{5,13},{6,22},{7,15},{8,24},{9,1... | collective-permute-start | bytes 393224 | tf_op jit(solution)/shard_map/ppermute | solution.py:174
  23.6 0.1 collective-permute-start.7
  23.7 2.0 %toeplitz_tiles.2.tiles_ref = bf16[8,16,128,128]{3,2,1,0:T(8,128)(2,1)S(1)} custom-call(f32[312,128]{1,0:T(8,128)S(1)} %strain_levels.1.flipped_ref), custom_call_target="tpu_custom_call" | custom-call | flops 134217728 | bytes 4194304 | tf_op jit(solution)/shard_map/toeplitz_tiles/pallas_call | solution.py:447
  25.7 0.8 %collective-permute-done.3 = f32[256,128]{1,0:T(8,128)S(1)} collective-permute-done((f32[256,128]{1,0:T(8,128)S(1)}, f32[256,128]{1,0:T(8,128)S(1)}, u32[]{:S(2)}, u32[]{:S(2)}) %collective-permute-start.3) | collective-permute-done | bytes 131104 | tf_op jit(solution)/shard_map/ppermute | solution.py:174
  26.5 2.1 %collective-permute-start.4 = (f32[256,128]{1,0:T(8,128)S(1)}, f32[256,128]{1,0:T(8,128)S(1)}, u32[]{:S(2)}, u32[]{:S(2)}) collective-permute-start(f32[256,128]{1,0:T(8,128)S(1)} %bitcast_add_fusion.3), channel_id=1, source_target_pairs={{0,2},{1,5},{2,0},{3,7},{4,6},{5,1},{6,4},{7,3},{8,10},{9,13},{10,... | collective-permute-start | bytes 393224 | tf_op jit(solution)/shard_map/ppermute | solution.py:182
  28.7 0.0 collective-permute-done.7
  28.7 1.6 %collective-permute-start.8 = (f32[256,128]{1,0:T(8,128)S(1)}, f32[256,128]{1,0:T(8,128)S(1)}, u32[]{:S(2)}, u32[]{:S(2)}) collective-permute-start(f32[256,128]{1,0:T(8,128)S(1)} %bitcast_add_fusion.2), channel_id=1, source_target_pairs={{0,2},{1,5},{2,0},{3,7},{4,6},{5,1},{6,4},{7,3},{8,10},{9,13},{10,... | collective-permute-start | bytes 393224 | tf_op jit(solution)/shard_map/ppermute | solution.py:182
  30.3 2.2 %toeplitz_tiles.3.tiles_ref = bf16[8,19,128,128]{3,2,1,0:T(8,128)(2,1)S(1)} custom-call(f32[312,128]{1,0:T(8,128)S(1)} %strain_levels.1.flipped_ref), custom_call_target="tpu_custom_call" | custom-call | flops 159383552 | bytes 4980736 | tf_op jit(solution)/shard_map/toeplitz_tiles/pallas_call | solution.py:447
  32.5 0.1 collective-permute-done.4
  32.6 3.0 %collective-permute-start.5 = (f32[256,128]{1,0:T(8,128)S(1)}, f32[256,128]{1,0:T(8,128)S(1)}, u32[]{:S(2)}, u32[]{:S(2)}) collective-permute-start(f32[256,128]{1,0:T(8,128)S(1)} %add.103), channel_id=1, source_target_pairs={{0,4},{1,3},{2,6},{3,1},{4,0},{5,7},{6,2},{7,5},{8,12},{9,11},{10,... | collective-permute-start | bytes 393224 | tf_op jit(solution)/shard_map/ppermute | solution.py:182
  35.6 0.0 collective-permute-done.8
  35.6 2.7 %collective-permute-start.9 = (f32[256,128]{1,0:T(8,128)S(1)}, f32[256,128]{1,0:T(8,128)S(1)}, u32[]{:S(2)}, u32[]{:S(2)}) collective-permute-start(f32[256,128]{1,0:T(8,128)S(1)} %add.109), channel_id=1, source_target_pairs={{0,4},{1,3},{2,6},{3,1},{4,0},{5,7},{6,2},{7,5},{8,12},{9,11},{10,... | collective-permute-start | bytes 393224 | tf_op jit(solution)/shard_map/ppermute | solution.py:182
  38.3 0.4 collective-permute-done.5
  38.7 0.1 collective-permute-start.6
  38.8 4.0 %collective-permute-done.9 = f32[256,128]{1,0:T(8,128)S(1)} collective-permute-done((f32[256,128]{1,0:T(8,128)S(1)}, f32[256,128]{1,0:T(8,128)S(1)}, u32[]{:S(2)}, u32[]{:S(2)}) %collective-permute-start.9) | collective-permute-done | bytes 131104 | tf_op jit(solution)/shard_map/ppermute | solution.py:182
  42.8 0.1 collective-permute-start.10
  42.8 0.0 collective-permute-done.6.other_ref
  42.8 3.7 %basis_first.1 = (f32[512,128]{1,0:T(8,128)S(1)}, f32[1,128]{1,0:T(1,128)S(1)}) custom-call(f32[256,128]{1,0:T(8,128)S(1)} %add.104.mine_ref, f32[256,128]{1,0:T(8,128)S(1)} %collective-permute-done.6.other_ref), custom_call_target="tpu_custom_call" | custom-call | tf_op jit(solution)/shard_map/basis_first/pallas_call | solution.py:301
  46.5 0.0 collective-permute-done.10.other_ref
  46.5 4.9 %basis_second.1 = (bf16[512,256]{1,0:T(8,128)(2,1)S(1)}, bf16[256,256]{1,0:T(8,128)(2,1)S(1)}, bf16[640,256]{1,0:T(8,128)(2,1)S(1)}, f32[1,256]{1,0:T(1,128)}) custom-call(f32[512,128]{1,0:T(8,128)S(1)} %get-tuple-element.43.first_ref, f32[1,128]{1,0:T(1,128)S(1)} %get-tuple-element.44.first_spectrum_ref, f32[256,128]{1,0:T(8,128)S(1)} %add.110.mine_ref, ...), custom_call_target="tpu_custom_call" | custom-call | tf_op jit(solution)/shard_map/basis_second/pallas_call | solution.py:341
  51.4 4.0 %collective-permute-start.12 = (bf16[256,256]{1,0:T(8,128)(2,1)S(1)}, bf16[256,256]{1,0:T(8,128)(2,1)S(1)}, u32[]{:S(2)}, u32[]{:S(2)}) collective-permute-start(bf16[256,256]{1,0:T(8,128)(2,1)S(1)} %get-tuple-element.54), channel_id=1, source_target_pairs={{0,24},{1,25},{2,26},{3,27},{4,28},{5,29},{6,30},{7,31},{8,16},{9,... | collective-permute-start | bytes 393224 | tf_op jit(solution)/shard_map/ppermute | solution.py:174
  55.4 0.5 collective-permute-start.11
  55.9 5.6 %filter_levels.2 = bf16[1,2,8192,256]{3,2,1,0:T(8,128)(2,1)} custom-call(bf16[8,19,128,128]{3,2,1,0:T(8,128)(2,1)S(1)} %toeplitz_tiles.3.tiles_ref, bf16[512,256]{1,0:T(8,128)(2,1)S(1)} %get-tuple-element.52.taps_ref.own_ref), custom_call_target="tpu_custom_call" | custom-call | flops 4294967296 | bytes 13369344 | tf_op jit(solution)/shard_map/filter_levels/pallas_call | solution.py:506
  61.5 0.0 copy-start
  61.5 0.0 copy-start.2
  61.5 0.0 collective-permute-done.12
  61.5 1.1 %collective-permute-done.11 = bf16[512,256]{1,0:T(8,128)(2,1)S(1)} collective-permute-done((bf16[512,256]{1,0:T(8,128)(2,1)S(1)}, bf16[512,256]{1,0:T(8,128)(2,1)S(1)}, u32[]{:S(2)}, u32[]{:S(2)}) %collective-permute-start.11) | collective-permute-done | bytes 262176 | tf_op jit(solution)/shard_map/ppermute | solution.py:174
  62.7 0.1 collective-permute-start.13
  62.7 3.7 %filter_levels.3 = (bf16[1,2,4096,256]{3,2,1,0:T(8,128)(2,1)}, bf16[1,2,2048,256]{3,2,1,0:T(8,128)(2,1)}, bf16[1,2,1024,256]{3,2,1,0:T(8,128)(2,1)}, bf16[1,2,512,256]{3,2,1,0:T(8,128)(2,1)}) custom-call(bf16[8,16,128,128]{3,2,1,0:T(8,128)(2,1)S(1)} %toeplitz_tiles.2.tiles_ref, bf16[640,256]{1,0:T(8,128)(2,1)S(1)} %get-tuple-element.62.taps_ref), custom_call_target="tpu_custom_call" | custom-call | flops 1543503872 | bytes 12058624 | tf_op jit(solution)/shard_map/filter_levels/pallas_call | solution.py:506
  66.4 0.0 collective-permute-done.13.other_ref
  66.4 0.0 copy-done
  66.4 0.0 copy-done.2
  66.5 2.4 %mixing.1 = bf16[1024,256]{1,0:T(8,128)(2,1)} custom-call(s32[1,1024]{1,0:T(1,128)S(1)} %bitcast.23, bf16[1024,512]{1,0:T(8,128)(2,1)S(1)} %copy-done, bf16[512,256]{1,0:T(8,128)(2,1)S(1)} %get-tuple-element.52.taps_ref.own_ref, bf16[768,256]{1,0:T(8,128)(2,1)S(1)} %constant_dynamic-update-slice_fusion.mine_ref, ...), custom_call_target="tpu_custom_call" | custom-call | tf_op jit(solution)/shard_map/mixing/pallas_call | solution.py:562
  (12 shorter events, 0.2 us)
Async XLA Ops:
  0.6 13.5 %copy-start.1 = (f32[2,8192]{1,0:T(2,128)S(1)}, f32[2,8192]{1,0:T(2,128)}, u32[]{:S(2)}) copy-start(f32[2,8192]{1,0:T(2,128)} %strain_ref.1) | copy-start | bytes 196612
  8.1 3.0 %collective-permute-start = (f32[2,2,2,256,128]{4,3,2,1,0:T(8,128)}, f32[2,2,2,256,128]{4,3,2,1,0:T(8,128)S(1)}, u32[]{:S(2)}, u32[]{:S(2)}) collective-permute-start(f32[2,2,2,256,128]{4,3,2,1,0:T(8,128)} %get-tuple-element.40), channel_id=1, source_target_pairs={{0,1},{1,0},{2,3},{3,2},{4,5},{5,4},{6,7},{7,6},{8,9},{9,8},{10,11... | collective-permute-start | bytes 3145736 | tf_op jit(solution)/shard_map/ppermute | solution.py:178
  11.2 10.1 %collective-permute-start.1 = (f32[2,2,256,128]{3,2,1,0:T(8,128)S(1)}, f32[2,2,256,128]{3,2,1,0:T(8,128)S(1)}, u32[]{:S(2)}, u32[]{:S(2)}) collective-permute-start(f32[2,2,256,128]{3,2,1,0:T(8,128)S(1)} %pad_maximum_fusion), channel_id=1, source_target_pairs={{0,8},{1,17},{2,10},{3,19},{4,12},{5,21},{6,14},{7,23},{8,0},{9,25... | collective-permute-start | bytes 1572872 | tf_op jit(solution)/shard_map/ppermute | solution.py:174
  14.2 2.6 %collective-permute-start.2 = (f32[2,2048]{1,0:T(2,128)S(1)}, f32[2,2048]{1,0:T(2,128)S(1)}, u32[]{:S(2)}, u32[]{:S(2)}) collective-permute-start(f32[2,2048]{1,0:T(2,128)S(1)} %slice.29), channel_id=1, source_target_pairs={{0,1},{1,2},{2,3},{3,4},{4,5},{5,6},{6,7},{8,9},{9,10},{10,11},{11... | collective-permute-start | bytes 49160 | tf_op jit(solution)/shard_map/ppermute | solution.py:595
  21.4 5.1 %collective-permute-start.3 = (f32[256,128]{1,0:T(8,128)S(1)}, f32[256,128]{1,0:T(8,128)S(1)}, u32[]{:S(2)}, u32[]{:S(2)}) collective-permute-start(f32[256,128]{1,0:T(8,128)S(1)} %dynamic-slice_bitcast_fusion.1), channel_id=1, source_target_pairs={{0,16},{1,9},{2,18},{3,11},{4,20},{5,13},{6,22},{7,15},{8,24},{9,1... | collective-permute-start | bytes 393224 | tf_op jit(solution)/shard_map/ppermute | solution.py:174
  23.6 5.1 %collective-permute-start.7 = (f32[256,128]{1,0:T(8,128)S(1)}, f32[256,128]{1,0:T(8,128)S(1)}, u32[]{:S(2)}, u32[]{:S(2)}) collective-permute-start(f32[256,128]{1,0:T(8,128)S(1)} %dynamic-slice_bitcast_fusion), channel_id=1, source_target_pairs={{0,16},{1,9},{2,18},{3,11},{4,20},{5,13},{6,22},{7,15},{8,24},{9,1... | collective-permute-start | bytes 393224 | tf_op jit(solution)/shard_map/ppermute | solution.py:174
  26.5 6.1 %collective-permute-start.4 = (f32[256,128]{1,0:T(8,128)S(1)}, f32[256,128]{1,0:T(8,128)S(1)}, u32[]{:S(2)}, u32[]{:S(2)}) collective-permute-start(f32[256,128]{1,0:T(8,128)S(1)} %bitcast_add_fusion.3), channel_id=1, source_target_pairs={{0,2},{1,5},{2,0},{3,7},{4,6},{5,1},{6,4},{7,3},{8,10},{9,13},{10,... | collective-permute-start | bytes 393224 | tf_op jit(solution)/shard_map/ppermute | solution.py:182
  28.7 6.9 %collective-permute-start.8 = (f32[256,128]{1,0:T(8,128)S(1)}, f32[256,128]{1,0:T(8,128)S(1)}, u32[]{:S(2)}, u32[]{:S(2)}) collective-permute-start(f32[256,128]{1,0:T(8,128)S(1)} %bitcast_add_fusion.2), channel_id=1, source_target_pairs={{0,2},{1,5},{2,0},{3,7},{4,6},{5,1},{6,4},{7,3},{8,10},{9,13},{10,... | collective-permute-start | bytes 393224 | tf_op jit(solution)/shard_map/ppermute | solution.py:182
  32.6 6.0 %collective-permute-start.5 = (f32[256,128]{1,0:T(8,128)S(1)}, f32[256,128]{1,0:T(8,128)S(1)}, u32[]{:S(2)}, u32[]{:S(2)}) collective-permute-start(f32[256,128]{1,0:T(8,128)S(1)} %add.103), channel_id=1, source_target_pairs={{0,4},{1,3},{2,6},{3,1},{4,0},{5,7},{6,2},{7,5},{8,12},{9,11},{10,... | collective-permute-start | bytes 393224 | tf_op jit(solution)/shard_map/ppermute | solution.py:182
  35.6 7.1 %collective-permute-start.9 = (f32[256,128]{1,0:T(8,128)S(1)}, f32[256,128]{1,0:T(8,128)S(1)}, u32[]{:S(2)}, u32[]{:S(2)}) collective-permute-start(f32[256,128]{1,0:T(8,128)S(1)} %add.109), channel_id=1, source_target_pairs={{0,4},{1,3},{2,6},{3,1},{4,0},{5,7},{6,2},{7,5},{8,12},{9,11},{10,... | collective-permute-start | bytes 393224 | tf_op jit(solution)/shard_map/ppermute | solution.py:182
  38.7 4.1 %collective-permute-start.6 = (f32[256,128]{1,0:T(8,128)S(1)}, f32[256,128]{1,0:T(8,128)S(1)}, u32[]{:S(2)}, u32[]{:S(2)}) collective-permute-start(f32[256,128]{1,0:T(8,128)S(1)} %add.104.mine_ref), channel_id=1, source_target_pairs={{0,1},{1,0},{2,3},{3,2},{4,5},{5,4},{6,7},{7,6},{8,9},{9,8},{10,11... | collective-permute-start | bytes 393224 | tf_op jit(solution)/shard_map/ppermute | solution.py:178
  42.8 3.8 %collective-permute-start.10 = (f32[256,128]{1,0:T(8,128)S(1)}, f32[256,128]{1,0:T(8,128)S(1)}, u32[]{:S(2)}, u32[]{:S(2)}) collective-permute-start(f32[256,128]{1,0:T(8,128)S(1)} %add.110.mine_ref), channel_id=1, source_target_pairs={{0,1},{1,0},{2,3},{3,2},{4,5},{5,4},{6,7},{7,6},{8,9},{9,8},{10,11... | collective-permute-start | bytes 393224 | tf_op jit(solution)/shard_map/ppermute | solution.py:178
  51.4 10.1 %collective-permute-start.12 = (bf16[256,256]{1,0:T(8,128)(2,1)S(1)}, bf16[256,256]{1,0:T(8,128)(2,1)S(1)}, u32[]{:S(2)}, u32[]{:S(2)}) collective-permute-start(bf16[256,256]{1,0:T(8,128)(2,1)S(1)} %get-tuple-element.54), channel_id=1, source_target_pairs={{0,24},{1,25},{2,26},{3,27},{4,28},{5,29},{6,30},{7,31},{8,16},{9,... | collective-permute-start | bytes 393224 | tf_op jit(solution)/shard_map/ppermute | solution.py:174
  55.4 7.2 %collective-permute-start.11 = (bf16[512,256]{1,0:T(8,128)(2,1)S(1)}, bf16[512,256]{1,0:T(8,128)(2,1)S(1)}, u32[]{:S(2)}, u32[]{:S(2)}) collective-permute-start(bf16[512,256]{1,0:T(8,128)(2,1)S(1)} %get-tuple-element.52.taps_ref.own_ref), channel_id=1, source_target_pairs={{0,8},{1,17},{2,10},{3,19},{4,12},{5,21},{6,14},{7,23},{8,0},{9,25... | collective-permute-start | bytes 786440 | tf_op jit(solution)/shard_map/ppermute | solution.py:174
  61.5 5.0 %copy-start = (bf16[1024,512]{1,0:T(8,128)(2,1)S(1)}, bf16[1024,512]{1,0:T(8,128)(2,1)}, u32[]{:S(2)}) copy-start(bf16[1024,512]{1,0:T(8,128)(2,1)} %get-tuple-element.37.white_ref) | copy-start | bytes 3145732
  61.5 5.0 %copy-start.2 = (s32[1024,1]{0,1:T(1,128)S(1)}, s32[1024,1]{0,1:T(1,128)}, u32[]{:S(2)}) copy-start(s32[1024,1]{0,1:T(1,128)} %param.7) | copy-start | bytes 12292
  62.7 3.8 %collective-permute-start.13 = (bf16[768,256]{1,0:T(8,128)(2,1)S(1)}, bf16[768,256]{1,0:T(8,128)(2,1)S(1)}, u32[]{:S(2)}, u32[]{:S(2)}) collective-permute-start(bf16[768,256]{1,0:T(8,128)(2,1)S(1)} %constant_dynamic-update-slice_fusion.mine_ref), channel_id=1, source_target_pairs={{0,1},{1,0},{2,3},{3,2},{4,5},{5,4},{6,7},{7,6},{8,9},{9,8},{10,11... | collective-permute-start | bytes 1179656 | tf_op jit(solution)/shard_map/ppermute | solution.py:178

commit v4 on v3

--- a/solution.py
+++ b/solution.py
@@ -59,7 +59,7 @@
                sem, out_sem):
     rows, width = templates_ref.shape
     rates = gains_ref.shape[0]
-    pieces = 4
+    pieces = 2
     piece = rows // pieces
     copies = [
         pltpu.make_async_copy(gains_hbm, gains_ref, sem.at[0]),
@@ -210,11 +210,11 @@
     )
     bits = [1 << i for i in range((grp // 2).bit_length() - 1)]
     mine[-1], *done = lax.optimization_barrier((mine[-1], *done))
-    mine[-1], done = beside[3](mine[-1], done)
     for step, bit in enumerate(bits):
+        if step == len(bits) - 1:
+            mine[-1], done = beside[3](mine[-1], done)
         mine = stage(mine, mine, lambda x: flip_chip(x, (bit, bits[-1 - step]), grp))
-        if step == 0:
-            mine[-1], *done = lax.optimization_barrier((mine[-1], *done))
+    mine[-1], *done = lax.optimization_barrier((mine[-1], *done))
     return mine, [flip_core(x, grp) for x in mine], done
 
 

time: 69.3 us -> 68.9 us (level)
  transfers between devices with their start and end apart: 14 -> 14, of which waited for: 8 -> 7; matrix products, arithmetic and copies ran while one was open for 2% -> 2% of each run, Pallas kernels for 26% -> 26%
where the time goes in v4:
time: 68.9 us; the launch traced here: 68.6 us
  Pallas kernels  32.4 us (47%)
  starting transfers between devices  21.5 us (31%)
  waiting for transfers between devices  11.9 us (17%)
  local copies, waits for them, and re-layouts  1.41 us (2%)
  between operations  1.05 us (2%)
    ppermute x5, starting transfers between devices, flip_bin(): return lax.ppermute(x, ('bin', 'grp'), pairs)  9.7 us
    ppermute x4, starting transfers between devices, flip_chip(): lax.ppermute(x, 'grp', [(i, i ^ 2 * bits[i % 2]) for i in range(grp)])  9.35 us
    pallas_call x2, Pallas kernels, filter_levels(): pl.pallas_call(functools.partial(filter_body, blocks, chunks), out_shape=...  9.24 us
    pallas_call x1, Pallas kernels, front(): pl.pallas_call(functools.partial(front_body, bins, grp), out_shape=(jax.S...  7.03 us
    ppermute x5, waiting for transfers between devices, flip_bin(): return lax.ppermute(x, ('bin', 'grp'), pairs)  5.42 us
    pallas_call x1, Pallas kernels, find_basis(): pl.pallas_call(functools.partial(basis_body, scale_down), out_shape=(jax....  4.86 us
    ppermute x4, waiting for transfers between devices, flip_chip(): lax.ppermute(x, 'grp', [(i, i ^ 2 * bits[i % 2]) for i in range(grp)])  4.46 us
    pallas_call x2, Pallas kernels, make_tiles(): pl.pallas_call(functools.partial(tiles_body, wanted, total, levels, block...  4.23 us
  transfers between devices with their start and end apart: 14, of which 7 were waited for; matrix products, arithmetic and copies ran while one was open for 2% of the time, Pallas kernels for 26%

profile of v4, /device:TPU:0, one launch (start us, length us, event | category | flops | bytes accessed | tf_op | source)
XLA Modules:
  0.0 68.6 jit_solution(531621303699598715)
XLA Ops:
  0.6 0.0 copy-start.1
  0.6 7.0 %whiten_products.1 = (bf16[1024,512]{1,0:T(8,128)(2,1)}, f32[2,2,2,256,128]{4,3,2,1,0:T(8,128)}, f32[2,2,2,256,128]{4,3,2,1,0:T(8,128)}) custom-call(s32[1,1024]{1,0:T(1,128)} %bitcast.22, s32[1,1024]{1,0:T(1,128)} %bitcast.24, f32[5,512]{1,0:T(8,128)} %gains_hbm.1, bf16[1024,512]{1,0:T(8,128)(2,1)} %templates_hbm.1, f32[512,256]{1,0:T(8,128)} %sketch_hbm.1), custom_call_target="tpu_custom_call" | custom-call | tf_op jit(solution)/shard_map/whiten_products/pallas_call | solution.py:141
  7.7 0.5 collective-permute-start
  8.2 1.3 %fusion = (f32[1,2,2,256,128]{4,3,2,1,0:T(8,128)S(1)}, f32[1,2,2,256,128]{4,3,2,1,0:T(8,128)S(1)}) fusion(f32[2,2,2,256,128]{4,3,2,1,0:T(8,128)} %get-tuple-element.42), kind=kLoop, calls=%fused_computation.11 | loop fusion | bytes 2097152 | tf_op jit(solution)/shard_map/slice | solution.py:204
  9.5 1.2 %collective-permute-done = f32[2,2,2,256,128]{4,3,2,1,0:T(8,128)S(1)} collective-permute-done((f32[2,2,2,256,128]{4,3,2,1,0:T(8,128)}, f32[2,2,2,256,128]{4,3,2,1,0:T(8,128)S(1)}, u32[]{:S(2)}, u32[]{:S(2)}) %collective-permute-start) | collective-permute-done | bytes 1048608 | tf_op jit(solution)/shard_map/ppermute | solution.py:178
  10.7 0.1 fusion.1
  10.7 0.1 add_bitcast_fusion
  10.9 2.9 %collective-permute-start.1 = (f32[2,2,256,128]{3,2,1,0:T(8,128)S(1)}, f32[2,2,256,128]{3,2,1,0:T(8,128)S(1)}, u32[]{:S(2)}, u32[]{:S(2)}) collective-permute-start(f32[2,2,256,128]{3,2,1,0:T(8,128)S(1)} %pad_maximum_fusion), channel_id=1, source_target_pairs={{0,8},{1,17},{2,10},{3,19},{4,12},{5,21},{6,14},{7,23},{8,0},{9,25... | collective-permute-start | bytes 1572872 | tf_op jit(solution)/shard_map/ppermute | solution.py:174
  13.8 0.0 copy-done.1
  13.8 1.8 %collective-permute-start.2 = (f32[2,2048]{1,0:T(2,128)S(1)}, f32[2,2048]{1,0:T(2,128)S(1)}, u32[]{:S(2)}, u32[]{:S(2)}) collective-permute-start(f32[2,2048]{1,0:T(2,128)S(1)} %slice.29), channel_id=1, source_target_pairs={{0,1},{1,2},{2,3},{3,4},{4,5},{5,6},{6,7},{8,9},{9,10},{10,11},{11... | collective-permute-start | bytes 49160 | tf_op jit(solution)/shard_map/ppermute | solution.py:595
  15.6 0.8 %collective-permute-done.2.history_ref = f32[2,2048]{1,0:T(2,128)S(1)} collective-permute-done((f32[2,2048]{1,0:T(2,128)S(1)}, f32[2,2048]{1,0:T(2,128)S(1)}, u32[]{:S(2)}, u32[]{:S(2)}) %collective-permute-start.2) | collective-permute-done | bytes 16416 | tf_op jit(solution)/shard_map/ppermute | solution.py:595
  16.4 1.0 %strain_levels.1.flipped_ref = f32[312,128]{1,0:T(8,128)S(1)} custom-call(f32[2,2048]{1,0:T(2,128)S(1)} %collective-permute-done.2.history_ref, f32[2,8192]{1,0:T(2,128)S(1)} %copy-done.1), custom_call_target="tpu_custom_call" | custom-call | tf_op jit(solution)/shard_map/strain_levels/pallas_call | solution.py:406
  17.5 3.5 %collective-permute-done.1 = f32[2,2,256,128]{3,2,1,0:T(8,128)S(1)} collective-permute-done((f32[2,2,256,128]{3,2,1,0:T(8,128)S(1)}, f32[2,2,256,128]{3,2,1,0:T(8,128)S(1)}, u32[]{:S(2)}, u32[]{:S(2)}) %collective-permute-start.1) | collective-permute-done | bytes 524320 | tf_op jit(solution)/shard_map/ppermute | solution.py:174
  21.0 0.1 bitcast_add_fusion
  21.1 2.1 %collective-permute-start.3 = (f32[256,128]{1,0:T(8,128)S(1)}, f32[256,128]{1,0:T(8,128)S(1)}, u32[]{:S(2)}, u32[]{:S(2)}) collective-permute-start(f32[256,128]{1,0:T(8,128)S(1)} %dynamic-slice_bitcast_fusion.1), channel_id=1, source_target_pairs={{0,16},{1,9},{2,18},{3,11},{4,20},{5,13},{6,22},{7,15},{8,24},{9,1... | collective-permute-start | bytes 393224 | tf_op jit(solution)/shard_map/ppermute | solution.py:174
  23.2 0.1 collective-permute-start.7
  23.3 2.0 %toeplitz_tiles.2.tiles_ref = bf16[8,16,128,128]{3,2,1,0:T(8,128)(2,1)S(1)} custom-call(f32[312,128]{1,0:T(8,128)S(1)} %strain_levels.1.flipped_ref), custom_call_target="tpu_custom_call" | custom-call | flops 134217728 | bytes 4194304 | tf_op jit(solution)/shard_map/toeplitz_tiles/pallas_call | solution.py:447
  25.3 0.8 %collective-permute-done.3 = f32[256,128]{1,0:T(8,128)S(1)} collective-permute-done((f32[256,128]{1,0:T(8,128)S(1)}, f32[256,128]{1,0:T(8,128)S(1)}, u32[]{:S(2)}, u32[]{:S(2)}) %collective-permute-start.3) | collective-permute-done | bytes 131104 | tf_op jit(solution)/shard_map/ppermute | solution.py:174
  26.2 2.1 %collective-permute-start.4 = (f32[256,128]{1,0:T(8,128)S(1)}, f32[256,128]{1,0:T(8,128)S(1)}, u32[]{:S(2)}, u32[]{:S(2)}) collective-permute-start(f32[256,128]{1,0:T(8,128)S(1)} %bitcast_add_fusion.3), channel_id=1, source_target_pairs={{0,2},{1,5},{2,0},{3,7},{4,6},{5,1},{6,4},{7,3},{8,10},{9,13},{10,... | collective-permute-start | bytes 393224 | tf_op jit(solution)/shard_map/ppermute | solution.py:182
  28.3 0.0 collective-permute-done.7
  28.3 1.6 %collective-permute-start.8 = (f32[256,128]{1,0:T(8,128)S(1)}, f32[256,128]{1,0:T(8,128)S(1)}, u32[]{:S(2)}, u32[]{:S(2)}) collective-permute-start(f32[256,128]{1,0:T(8,128)S(1)} %bitcast_add_fusion.2), channel_id=1, source_target_pairs={{0,2},{1,5},{2,0},{3,7},{4,6},{5,1},{6,4},{7,3},{8,10},{9,13},{10,... | collective-permute-start | bytes 393224 | tf_op jit(solution)/shard_map/ppermute | solution.py:182
  29.9 2.3 %collective-permute-done.4 = f32[256,128]{1,0:T(8,128)S(1)} collective-permute-done((f32[256,128]{1,0:T(8,128)S(1)}, f32[256,128]{1,0:T(8,128)S(1)}, u32[]{:S(2)}, u32[]{:S(2)}) %collective-permute-start.4) | collective-permute-done | bytes 131104 | tf_op jit(solution)/shard_map/ppermute | solution.py:182
  32.3 3.0 %collective-permute-start.5 = (f32[256,128]{1,0:T(8,128)S(1)}, f32[256,128]{1,0:T(8,128)S(1)}, u32[]{:S(2)}, u32[]{:S(2)}) collective-permute-start(f32[256,128]{1,0:T(8,128)S(1)} %add.103), channel_id=1, source_target_pairs={{0,4},{1,3},{2,6},{3,1},{4,0},{5,7},{6,2},{7,5},{8,12},{9,11},{10,... | collective-permute-start | bytes 393224 | tf_op jit(solution)/shard_map/ppermute | solution.py:182
  35.2 0.0 collective-permute-done.8
  35.2 2.7 %collective-permute-start.9 = (f32[256,128]{1,0:T(8,128)S(1)}, f32[256,128]{1,0:T(8,128)S(1)}, u32[]{:S(2)}, u32[]{:S(2)}) collective-permute-start(f32[256,128]{1,0:T(8,128)S(1)} %add.109), channel_id=1, source_target_pairs={{0,4},{1,3},{2,6},{3,1},{4,0},{5,7},{6,2},{7,5},{8,12},{9,11},{10,... | collective-permute-start | bytes 393224 | tf_op jit(solution)/shard_map/ppermute | solution.py:182
  37.9 2.2 %toeplitz_tiles.3.tiles_ref = bf16[8,19,128,128]{3,2,1,0:T(8,128)(2,1)S(1)} custom-call(f32[312,128]{1,0:T(8,128)S(1)} %strain_levels.1.flipped_ref), custom_call_target="tpu_custom_call" | custom-call | flops 159383552 | bytes 4980736 | tf_op jit(solution)/shard_map/toeplitz_tiles/pallas_call | solution.py:447
  40.1 0.0 collective-permute-done.5
  40.2 0.1 collective-permute-start.6
  40.2 2.1 %collective-permute-done.9 = f32[256,128]{1,0:T(8,128)S(1)} collective-permute-done((f32[256,128]{1,0:T(8,128)S(1)}, f32[256,128]{1,0:T(8,128)S(1)}, u32[]{:S(2)}, u32[]{:S(2)}) %collective-permute-start.9) | collective-permute-done | bytes 131104 | tf_op jit(solution)/shard_map/ppermute | solution.py:182
  42.4 0.1 collective-permute-start.10
  42.5 0.0 collective-permute-done.6.other_ref
  42.5 3.6 %basis_first.1 = (f32[512,128]{1,0:T(8,128)S(1)}, f32[1,128]{1,0:T(1,128)S(1)}) custom-call(f32[256,128]{1,0:T(8,128)S(1)} %add.104.mine_ref, f32[256,128]{1,0:T(8,128)S(1)} %collective-permute-done.6.other_ref), custom_call_target="tpu_custom_call" | custom-call | tf_op jit(solution)/shard_map/basis_first/pallas_call | solution.py:301
  46.1 0.0 collective-permute-done.10.other_ref
  46.1 4.9 %basis_second.1 = (bf16[512,256]{1,0:T(8,128)(2,1)S(1)}, bf16[256,256]{1,0:T(8,128)(2,1)S(1)}, bf16[640,256]{1,0:T(8,128)(2,1)S(1)}, f32[1,256]{1,0:T(1,128)}) custom-call(f32[512,128]{1,0:T(8,128)S(1)} %get-tuple-element.46.first_ref, f32[1,128]{1,0:T(1,128)S(1)} %get-tuple-element.47.first_spectrum_ref, f32[256,128]{1,0:T(8,128)S(1)} %add.110.mine_ref, ...), custom_call_target="tpu_custom_call" | custom-call | tf_op jit(solution)/shard_map/basis_second/pallas_call | solution.py:341
  51.0 4.0 %collective-permute-start.12 = (bf16[256,256]{1,0:T(8,128)(2,1)S(1)}, bf16[256,256]{1,0:T(8,128)(2,1)S(1)}, u32[]{:S(2)}, u32[]{:S(2)}) collective-permute-start(bf16[256,256]{1,0:T(8,128)(2,1)S(1)} %get-tuple-element.60), channel_id=1, source_target_pairs={{0,24},{1,25},{2,26},{3,27},{4,28},{5,29},{6,30},{7,31},{8,16},{9,... | collective-permute-start | bytes 393224 | tf_op jit(solution)/shard_map/ppermute | solution.py:174
  55.0 0.5 collective-permute-start.11
  55.5 5.6 %filter_levels.2 = bf16[1,2,8192,256]{3,2,1,0:T(8,128)(2,1)} custom-call(bf16[8,19,128,128]{3,2,1,0:T(8,128)(2,1)S(1)} %toeplitz_tiles.3.tiles_ref, bf16[512,256]{1,0:T(8,128)(2,1)S(1)} %get-tuple-element.58.taps_ref.own_ref), custom_call_target="tpu_custom_call" | custom-call | flops 4294967296 | bytes 13369344 | tf_op jit(solution)/shard_map/filter_levels/pallas_call | solution.py:506
  61.1 0.0 copy-start
  61.1 0.0 copy-start.2
  61.1 0.0 collective-permute-done.12
  61.1 1.1 %collective-permute-done.11 = bf16[512,256]{1,0:T(8,128)(2,1)S(1)} collective-permute-done((bf16[512,256]{1,0:T(8,128)(2,1)S(1)}, bf16[512,256]{1,0:T(8,128)(2,1)S(1)}, u32[]{:S(2)}, u32[]{:S(2)}) %collective-permute-start.11) | collective-permute-done | bytes 262176 | tf_op jit(solution)/shard_map/ppermute | solution.py:174
  62.3 0.1 collective-permute-start.13
  62.4 3.7 %filter_levels.3 = (bf16[1,2,4096,256]{3,2,1,0:T(8,128)(2,1)}, bf16[1,2,2048,256]{3,2,1,0:T(8,128)(2,1)}, bf16[1,2,1024,256]{3,2,1,0:T(8,128)(2,1)}, bf16[1,2,512,256]{3,2,1,0:T(8,128)(2,1)}) custom-call(bf16[8,16,128,128]{3,2,1,0:T(8,128)(2,1)S(1)} %toeplitz_tiles.2.tiles_ref, bf16[640,256]{1,0:T(8,128)(2,1)S(1)} %get-tuple-element.68.taps_ref), custom_call_target="tpu_custom_call" | custom-call | flops 1543503872 | bytes 12058624 | tf_op jit(solution)/shard_map/filter_levels/pallas_call | solution.py:506
  66.1 0.0 collective-permute-done.13.other_ref
  66.1 0.0 copy-done
  66.1 0.0 copy-done.2
  66.1 2.4 %mixing.1 = bf16[1024,256]{1,0:T(8,128)(2,1)} custom-call(s32[1,1024]{1,0:T(1,128)S(1)} %bitcast.23, bf16[1024,512]{1,0:T(8,128)(2,1)S(1)} %copy-done, bf16[512,256]{1,0:T(8,128)(2,1)S(1)} %get-tuple-element.58.taps_ref.own_ref, bf16[768,256]{1,0:T(8,128)(2,1)S(1)} %constant_dynamic-update-slice_fusion.mine_ref, ...), custom_call_target="tpu_custom_call" | custom-call | tf_op jit(solution)/shard_map/mixing/pallas_call | solution.py:562
  (12 shorter events, 0.2 us)
Async XLA Ops:
  0.6 13.2 %copy-start.1 = (f32[2,8192]{1,0:T(2,128)S(1)}, f32[2,8192]{1,0:T(2,128)}, u32[]{:S(2)}) copy-start(f32[2,8192]{1,0:T(2,128)} %strain_ref.1) | copy-start | bytes 196612
  7.7 3.0 %collective-permute-start = (f32[2,2,2,256,128]{4,3,2,1,0:T(8,128)}, f32[2,2,2,256,128]{4,3,2,1,0:T(8,128)S(1)}, u32[]{:S(2)}, u32[]{:S(2)}) collective-permute-start(f32[2,2,2,256,128]{4,3,2,1,0:T(8,128)} %get-tuple-element.43), channel_id=1, source_target_pairs={{0,1},{1,0},{2,3},{3,2},{4,5},{5,4},{6,7},{7,6},{8,9},{9,8},{10,11... | collective-permute-start | bytes 3145736 | tf_op jit(solution)/shard_map/ppermute | solution.py:178
  10.9 10.1 %collective-permute-start.1 = (f32[2,2,256,128]{3,2,1,0:T(8,128)S(1)}, f32[2,2,256,128]{3,2,1,0:T(8,128)S(1)}, u32[]{:S(2)}, u32[]{:S(2)}) collective-permute-start(f32[2,2,256,128]{3,2,1,0:T(8,128)S(1)} %pad_maximum_fusion), channel_id=1, source_target_pairs={{0,8},{1,17},{2,10},{3,19},{4,12},{5,21},{6,14},{7,23},{8,0},{9,25... | collective-permute-start | bytes 1572872 | tf_op jit(solution)/shard_map/ppermute | solution.py:174
  13.8 2.6 %collective-permute-start.2 = (f32[2,2048]{1,0:T(2,128)S(1)}, f32[2,2048]{1,0:T(2,128)S(1)}, u32[]{:S(2)}, u32[]{:S(2)}) collective-permute-start(f32[2,2048]{1,0:T(2,128)S(1)} %slice.29), channel_id=1, source_target_pairs={{0,1},{1,2},{2,3},{3,4},{4,5},{5,6},{6,7},{8,9},{9,10},{10,11},{11... | collective-permute-start | bytes 49160 | tf_op jit(solution)/shard_map/ppermute | solution.py:595
  21.1 5.1 %collective-permute-start.3 = (f32[256,128]{1,0:T(8,128)S(1)}, f32[256,128]{1,0:T(8,128)S(1)}, u32[]{:S(2)}, u32[]{:S(2)}) collective-permute-start(f32[256,128]{1,0:T(8,128)S(1)} %dynamic-slice_bitcast_fusion.1), channel_id=1, source_target_pairs={{0,16},{1,9},{2,18},{3,11},{4,20},{5,13},{6,22},{7,15},{8,24},{9,1... | collective-permute-start | bytes 393224 | tf_op jit(solution)/shard_map/ppermute | solution.py:174
  23.2 5.1 %collective-permute-start.7 = (f32[256,128]{1,0:T(8,128)S(1)}, f32[256,128]{1,0:T(8,128)S(1)}, u32[]{:S(2)}, u32[]{:S(2)}) collective-permute-start(f32[256,128]{1,0:T(8,128)S(1)} %dynamic-slice_bitcast_fusion), channel_id=1, source_target_pairs={{0,16},{1,9},{2,18},{3,11},{4,20},{5,13},{6,22},{7,15},{8,24},{9,1... | collective-permute-start | bytes 393224 | tf_op jit(solution)/shard_map/ppermute | solution.py:174
  26.2 6.1 %collective-permute-start.4 = (f32[256,128]{1,0:T(8,128)S(1)}, f32[256,128]{1,0:T(8,128)S(1)}, u32[]{:S(2)}, u32[]{:S(2)}) collective-permute-start(f32[256,128]{1,0:T(8,128)S(1)} %bitcast_add_fusion.3), channel_id=1, source_target_pairs={{0,2},{1,5},{2,0},{3,7},{4,6},{5,1},{6,4},{7,3},{8,10},{9,13},{10,... | collective-permute-start | bytes 393224 | tf_op jit(solution)/shard_map/ppermute | solution.py:182
  28.3 6.9 %collective-permute-start.8 = (f32[256,128]{1,0:T(8,128)S(1)}, f32[256,128]{1,0:T(8,128)S(1)}, u32[]{:S(2)}, u32[]{:S(2)}) collective-permute-start(f32[256,128]{1,0:T(8,128)S(1)} %bitcast_add_fusion.2), channel_id=1, source_target_pairs={{0,2},{1,5},{2,0},{3,7},{4,6},{5,1},{6,4},{7,3},{8,10},{9,13},{10,... | collective-permute-start | bytes 393224 | tf_op jit(solution)/shard_map/ppermute | solution.py:182
  32.3 7.9 %collective-permute-start.5 = (f32[256,128]{1,0:T(8,128)S(1)}, f32[256,128]{1,0:T(8,128)S(1)}, u32[]{:S(2)}, u32[]{:S(2)}) collective-permute-start(f32[256,128]{1,0:T(8,128)S(1)} %add.103), channel_id=1, source_target_pairs={{0,4},{1,3},{2,6},{3,1},{4,0},{5,7},{6,2},{7,5},{8,12},{9,11},{10,... | collective-permute-start | bytes 393224 | tf_op jit(solution)/shard_map/ppermute | solution.py:182
  35.2 7.1 %collective-permute-start.9 = (f32[256,128]{1,0:T(8,128)S(1)}, f32[256,128]{1,0:T(8,128)S(1)}, u32[]{:S(2)}, u32[]{:S(2)}) collective-permute-start(f32[256,128]{1,0:T(8,128)S(1)} %add.109), channel_id=1, source_target_pairs={{0,4},{1,3},{2,6},{3,1},{4,0},{5,7},{6,2},{7,5},{8,12},{9,11},{10,... | collective-permute-start | bytes 393224 | tf_op jit(solution)/shard_map/ppermute | solution.py:182
  40.2 2.3 %collective-permute-start.6 = (f32[256,128]{1,0:T(8,128)S(1)}, f32[256,128]{1,0:T(8,128)S(1)}, u32[]{:S(2)}, u32[]{:S(2)}) collective-permute-start(f32[256,128]{1,0:T(8,128)S(1)} %add.104.mine_ref), channel_id=1, source_target_pairs={{0,1},{1,0},{2,3},{3,2},{4,5},{5,4},{6,7},{7,6},{8,9},{9,8},{10,11... | collective-permute-start | bytes 393224 | tf_op jit(solution)/shard_map/ppermute | solution.py:178
  42.4 3.7 %collective-permute-start.10 = (f32[256,128]{1,0:T(8,128)S(1)}, f32[256,128]{1,0:T(8,128)S(1)}, u32[]{:S(2)}, u32[]{:S(2)}) collective-permute-start(f32[256,128]{1,0:T(8,128)S(1)} %add.110.mine_ref), channel_id=1, source_target_pairs={{0,1},{1,0},{2,3},{3,2},{4,5},{5,4},{6,7},{7,6},{8,9},{9,8},{10,11... | collective-permute-start | bytes 393224 | tf_op jit(solution)/shard_map/ppermute | solution.py:178
  51.0 10.1 %collective-permute-start.12 = (bf16[256,256]{1,0:T(8,128)(2,1)S(1)}, bf16[256,256]{1,0:T(8,128)(2,1)S(1)}, u32[]{:S(2)}, u32[]{:S(2)}) collective-permute-start(bf16[256,256]{1,0:T(8,128)(2,1)S(1)} %get-tuple-element.60), channel_id=1, source_target_pairs={{0,24},{1,25},{2,26},{3,27},{4,28},{5,29},{6,30},{7,31},{8,16},{9,... | collective-permute-start | bytes 393224 | tf_op jit(solution)/shard_map/ppermute | solution.py:174
  55.0 7.3 %collective-permute-start.11 = (bf16[512,256]{1,0:T(8,128)(2,1)S(1)}, bf16[512,256]{1,0:T(8,128)(2,1)S(1)}, u32[]{:S(2)}, u32[]{:S(2)}) collective-permute-start(bf16[512,256]{1,0:T(8,128)(2,1)S(1)} %get-tuple-element.58.taps_ref.own_ref), channel_id=1, source_target_pairs={{0,8},{1,17},{2,10},{3,19},{4,12},{5,21},{6,14},{7,23},{8,0},{9,25... | collective-permute-start | bytes 786440 | tf_op jit(solution)/shard_map/ppermute | solution.py:174
  61.1 5.0 %copy-start = (bf16[1024,512]{1,0:T(8,128)(2,1)S(1)}, bf16[1024,512]{1,0:T(8,128)(2,1)}, u32[]{:S(2)}) copy-start(bf16[1024,512]{1,0:T(8,128)(2,1)} %get-tuple-element.40.white_ref) | copy-start | bytes 3145732
  61.1 5.0 %copy-start.2 = (s32[1024,1]{0,1:T(1,128)S(1)}, s32[1024,1]{0,1:T(1,128)}, u32[]{:S(2)}) copy-start(s32[1024,1]{0,1:T(1,128)} %param.7) | copy-start | bytes 12292
  62.3 3.8 %collective-permute-start.13 = (bf16[768,256]{1,0:T(8,128)(2,1)S(1)}, bf16[768,256]{1,0:T(8,128)(2,1)S(1)}, u32[]{:S(2)}, u32[]{:S(2)}) collective-permute-start(bf16[768,256]{1,0:T(8,128)(2,1)S(1)} %constant_dynamic-update-slice_fusion.mine_ref), channel_id=1, source_target_pairs={{0,1},{1,0},{2,3},{3,2},{4,5},{5,4},{6,7},{7,6},{8,9},{9,8},{10,11... | collective-permute-start | bytes 1179656 | tf_op jit(solution)/shard_map/ppermute | solution.py:178
